TPU v7x, 32 devices: a whole 2x2x4 slice. The times are simulated.
32 devices in a mesh: tm: 8 (over z, x), lat: 4 (over y, core).
Axes of the slice: x: 2, y: 2, z: 4, core: 2. Of those that a mesh axis runs over, the one named last changes fastest.
Arguments:
- fields: bfloat16 [8, 720, 1440], P('tm', 'lat'), may hold values from -6 to 6
- legendre: bfloat16 [720, 720, 720], P('lat', 'tm'), may hold values from -0.21875 to 0.21875
- nugget: float32 [720, 720, 2], P('lat', 'tm'), may hold values from 0.2 to 2
- chosen: int32 [1024], replicated, may hold values from 0 to 1036799, as said below
Outputs:
- panels: bfloat16 [720, 720, 2, 1024], P('lat', 'tm')
Inputs may be any that keep to these rules, and one draw needn't show every extreme that they name: `chosen`: distinct flat indices (l * 720 + m) 2 + c with l >= m and not c = 1 at m = 0.
All inputs are finite; a program needn't handle non-finite values.
Results may differ from a plain program's by a relative error of at most 0.028.
Values may be sent and summed in bfloat16 or wider, within the bound.
No kernel may reach another device: no remote copies, remote signals or barrier semaphores. Data moves between devices by JAX's collectives and lax.ppermute only.
A program may use at most 448 MiB of HBM per device.

v0:
```python
import math

import jax
import jax.numpy as jnp
from jax import lax
from jax.sharding import PartitionSpec as P

ORD = 720


HIGH = lax.Precision.HIGHEST


def basis_table(count_lon, count_ord):
    cols = (
        jnp.arange(count_lon, dtype=jnp.int32)[:, None]
        * jnp.arange(count_ord, dtype=jnp.int32)[None, :]
    )
    angle = (cols % count_lon).astype(jnp.float32) * (2.0 * math.pi / count_lon)
    scale = 1.0 / math.sqrt(count_lon)
    table = jnp.stack([jnp.cos(angle) * scale, -jnp.sin(angle) * scale], axis=2)
    return table.reshape(count_lon, 2 * count_ord).astype(jnp.bfloat16)


def on_device(fields, legendre, nugget, chosen):
    t_local, lat_local, lon_count = fields.shape
    ord_local = legendre.shape[1]
    deg_count = legendre.shape[2]
    deg_local = nugget.shape[0]
    basis = basis_table(lon_count, ORD)
    spectra = jnp.dot(fields.reshape(-1, lon_count), basis, preferred_element_type=jnp.float32)
    spectra = spectra.astype(jnp.bfloat16).reshape(t_local, lat_local, 2 * ORD)
    moved = lax.all_to_all(spectra, "tm", split_axis=2, concat_axis=0, tiled=True)
    times = moved.shape[0]
    moved = moved.reshape(times, lat_local, ord_local, 2)
    moved = jnp.transpose(moved, (1, 2, 3, 0)).reshape(lat_local, ord_local, 2 * times)
    ord_start = lax.axis_index("tm") * ord_local
    ord_global = ord_start + jnp.arange(ord_local, dtype=jnp.int32)
    keep = jnp.arange(deg_count, dtype=jnp.int32)[None, :] >= ord_global[:, None]
    masked = jnp.where(keep[None], legendre, jnp.zeros_like(legendre))
    summed = lax.psum_scatter(
        jnp.einsum("jmx,jml->lmx", moved, masked, preferred_element_type=jnp.float32).astype(
            jnp.bfloat16
        ),
        "lat",
        scatter_dimension=0,
        tiled=True,
    )
    coef_rows = summed.reshape(deg_local * ord_local * 2, times)
    deg_start = lax.axis_index("lat") * deg_local
    deg_pick = chosen // (2 * ORD) - deg_start
    ord_pick = chosen // 2 % ORD - ord_start
    comp_pick = chosen % 2
    inside = (deg_pick >= 0) & (deg_pick < deg_local) & (ord_pick >= 0) & (ord_pick < ord_local)
    row_pick = jnp.where(inside, (deg_pick * ord_local + ord_pick) * 2 + comp_pick, 0)
    nug_rows = nugget.reshape(-1)
    picked_part = jnp.where(inside[None, :], coef_rows[row_pick].T.astype(jnp.float32), 0.0)
    nug_part = jnp.where(inside, nug_rows[row_pick], 0.0)
    picked, nug_sel = lax.psum((picked_part, nug_part), ("tm", "lat"))
    picked = picked.astype(jnp.bfloat16)
    panel = chosen.shape[0] // 2
    block = jnp.dot(picked.T, picked, preferred_element_type=jnp.float32) / times
    block = block + jnp.diag(nug_sel)
    eye = jnp.eye(panel, dtype=jnp.float32)
    l11 = jnp.linalg.cholesky(block[:panel, :panel])
    inv11 = jax.scipy.linalg.solve_triangular(l11, eye, lower=True)
    l21 = jnp.dot(block[panel:, :panel], inv11.T, precision=HIGH)
    l22 = jnp.linalg.cholesky(block[panel:, panel:] - jnp.dot(l21, l21.T, precision=HIGH))
    inv22 = jax.scipy.linalg.solve_triangular(l22, eye, lower=True)
    cov = jnp.dot(coef_rows, picked, preferred_element_type=jnp.float32) / times
    column_ids = jnp.arange(2 * panel, dtype=jnp.int32)
    cov = cov.at[row_pick, column_ids].add(jnp.where(inside, nug_rows[row_pick], 0.0))
    first = jnp.dot(cov[:, :panel], inv11.T, precision=HIGH)
    rest = cov[:, panel:] - jnp.dot(first, l21.T, precision=HIGH)
    second = jnp.dot(rest, inv22.T, precision=HIGH)
    joined = jnp.concatenate([first, second], axis=1).astype(jnp.bfloat16)
    return joined.reshape(deg_local, ord_local, 2, 2 * panel)


def solution(mesh):
    placed = (P("tm", "lat", None), P("lat", "tm", None), P("lat", "tm", None), P())
    return jax.shard_map(
        on_device, mesh=mesh, in_specs=placed, out_specs=P("lat", "tm", None, None), check_vma=False
    )
```

profile of v0, /device:TPU:0, one launch (start us, length us, event | category | flops | bytes accessed | tf_op | source)
XLA Modules:
  0.0 1520.6 jit_solution(1762913200459809945)
XLA Ops:
  6.5 19.1 %multiply_convert_fusion = (bf16[1440,720,1]{1,0,2:T(8,128)(2,1)S(1)}, bf16[1440,720,1]{1,0,2:T(8,128)(2,1)S(1)}) fusion(), kind=kLoop, calls=%fused_computation.22 | loop fusion | flops 14515200 | bytes 4147200 | tf_op jit(solution)/shard_map/convert.5
  28.2 12.6 copy.33
  40.8 9.9 convert_element_type.53
  75.2 13.7 all-to-all-done
  94.6 11.5 convert_bitcast_fusion
  124.8 34.0 %all-reduce.5.cloned.1.call-done = bf16[720,90,16]{0,2,1:T(8,128)(2,1)} async-done(((bf16[720,90,16]{0,2,1:T(8,128)(2,1)}), bf16[720,90,16]{0,2,1:T(8,128)(2,1)}) %all-reduce.5.cloned.1.call-update) | async-done | bytes 2073616
  164.6 10.8 reshape.154
  183.0 47.0 %all-reduce.2 = (bf16[8,1024]{0,1:T(8,128)(2,1)S(1)}, f32[1024]{0:T(1024)S(1)}) all-reduce(f32[8,1024]{0,1:T(8,128)S(1)} %select_bitcast_fusion, f32[1024]{0:T(1024)S(1)} %broadcast_select_fusion), channel_id=1, replica_groups=mesh['tm'=8,'lat'=4] {'tm','lat'}, use_global_device_ids=true, to_apply=%region_1.2 | all-reduce | flops 9216 | bytes 57344 | tf_op jit(solution)/shard_map/psum | solution.py:59
  237.8 11.7 cholesky.286
  262.8 11.7 cholesky.305
  275.1 10.2 custom-call.28
  286.9 11.7 cholesky.326
  299.3 9.8 custom-call.29
  310.6 11.9 cholesky.343
  326.9 11.7 while.4
  338.6 39.3 %custom-call.30 = f32[4,128,128]{1,2,0:T(8,128)S(1)} custom-call(f32[4,128,128]{2,1,0:T(8,128)S(1)} %get-tuple-element.21), custom_call_target="InvertDiagBlocksLowerTriangular" | custom-call | tf_op jit(solution)/shard_map/jit(_solve_triangular)/triangular_solve | solution.py:66
  389.6 47.9 %multiply_bitcast_fusion = f32[4050,8,8,128]{3,2,1,0:T(8,128)} fusion(bf16[32400,8]{1,0:T(8,128)(2,1)} %reshape.154, bf16[8,1024]{0,1:T(8,128)(2,1)S(1)} %get-tuple-element.39), kind=kOutput, calls=%fused_computation.7 | convolution fusion | flops 564019200 | bytes 133245184 | tf_op jit(solution)/shard_map/dot_general | solution.py:70
  445.7 11.7 cholesky.358
  470.6 11.9 cholesky.377
  494.5 11.7 cholesky.398
  518.2 11.9 cholesky.415
  534.4 11.7 while.5
  546.1 39.3 %custom-call.34 = f32[4,128,128]{1,2,0:T(8,128)S(1)} custom-call(f32[4,128,128]{2,1,0:T(8,128)S(1)} %get-tuple-element.22), custom_call_target="InvertDiagBlocksLowerTriangular" | custom-call | tf_op jit(solution)/shard_map/jit(_solve_triangular)/triangular_solve | solution.py:69
  592.3 87.4 %copy.47 = f32[4050,8,8,128]{3,1,2,0:T(8,128)} copy(f32[4050,8,8,128]{3,2,1,0:T(8,128)} %multiply_bitcast_fusion) | data formatting | bytes 265420800
  679.7 142.2 %scatter_fusion = f32[33177600]{0:T(1024)} fusion(f32[33177600]{0:T(1024)} %bitcast.46, s32[1024]{0:T(1024)S(1)} %broadcast_select_fusion.1, f32[1024]{0:T(1024)S(1)} %broadcast_select_fusion), kind=kCustom, calls=%fused_computation.2 | custom fusion | flops 1024 | bytes 16384
  821.9 140.0 %reshape.159 = f32[32400,1024]{1,0:T(8,128)} reshape(f32[33177600]{0:T(1024)} %scatter_fusion) | data formatting | bytes 265420800 | tf_op jit(solution)/shard_map/scatter-add | solution.py:72
  961.9 115.1 %fusion.102 = (bf16[32400,512]{1,0:T(8,128)(2,1)}, f32[32400,512]{1,0:T(8,128)}) fusion(f32[32400,1024]{1,0:T(8,128)} %reshape.159, f32[512,512]{1,0:T(8,128)S(1)} %copy-done.6), kind=kOutput, calls=%fused_computation.205 | convolution fusion | flops 101938176000 | bytes 166936576 | tf_op jit(solution)/shard_map/dot_general | solution.py:73
  1077.0 64.4 %concatenate.21 = bf16[180,90,2,512]{3,2,1,0:T(2,128)(2,1)} reshape(bf16[32400,512]{1,0:T(8,128)(2,1)} %get-tuple-element.72) | data formatting | bytes 66355200 | tf_op jit(solution)/shard_map/concatenate | solution.py:76
  1141.5 113.7 %fusion.103 = f32[32400,512]{1,0:T(8,128)} fusion(f32[32400,512]{1,0:T(8,128)} %get-tuple-element.73, f32[512,512]{1,0:T(8,128)S(1)} %copy-done.3), kind=kOutput, calls=%fused_computation.206 | convolution fusion | flops 101921587200 | bytes 133758976 | tf_op jit(solution)/shard_map/dot_general | solution.py:74
  1255.2 115.8 %fusion.3 = bf16[32400,512]{1,0:T(8,128)(2,1)} fusion(f32[32400,512]{1,0:T(8,128)} %fusion.103, f32[32400,1024]{1,0:T(8,128)} %reshape.159, f32[128,512]{1,0:T(8,128)S(1)} %copy-done.14, f32[128,512]{1,0:T(8,128)S(1)} %copy-done.13, f32[128,512]{1,0:T(8,128)S(1)} %copy-done.8, f32[128,512]{1,0:T(8,128)S(1)} %copy-done.5), kind=kOutput, calls=%fused_computation.13 | convolution fusion | flops 101955551232 | bytes 166936576 | tf_op jit(solution)/shard_map/dot_general | solution.py:75
  1370.9 64.3 %concatenate.22 = bf16[180,90,2,512]{3,2,1,0:T(2,128)(2,1)} reshape(bf16[32400,512]{1,0:T(8,128)(2,1)} %fusion.3) | data formatting | bytes 66355200 | tf_op jit(solution)/shard_map/concatenate | solution.py:76
  1435.2 78.3 %pad_maximum_fusion = bf16[180,90,2,1024]{3,2,1,0:T(2,128)(2,1)} fusion(bf16[180,90,2,512]{3,2,1,0:T(2,128)(2,1)} %concatenate.22, bf16[180,90,2,512]{3,2,1,0:T(2,128)(2,1)} %concatenate.21), kind=kLoop, calls=%fused_computation.12 | loop fusion | flops 132710400 | bytes 132710400 | tf_op jit(solution)/shard_map/concatenate | solution.py:76
  (163 shorter events, 179.8 us)
Async XLA Ops:
  6.5 44.1 %copy-start = (bf16[1,180,1440]{2,1,0:T(8,128)(2,1)S(1)}, bf16[1,180,1440]{2,1,0:T(8,128)(2,1)}, u32[]{:S(2)}) copy-start(bf16[1,180,1440]{2,1,0:T(8,128)(2,1)} %param.7) | copy-start | bytes 1555204
  67.2 21.7 %all-to-all-start = ((bf16[8,2,16200]{2,1,0:T(2,128)(2,1)}), bf16[8,2,16200]{2,1,0:T(2,128)(2,1)S(1)}, u32[]{:S(2)}, u32[]{:S(2)}) async-start(bf16[8,2,16200]{2,1,0:T(2,128)(2,1)} %reshape.209), calls=%async_computation | async-start | bytes 1040384 | tf_op jit(solution)/shard_map/all_to_all | solution.py:33
  74.5 84.4 %all-reduce.5.cloned.1.call-start = ((), (), s32[]{:S(2)}) async-start(), calls=%async_computation.1 | async-start | bytes 4423680
  94.6 11.6 copy-start.16
  94.6 11.6 copy-start.15
  111.3 5.8 copy-start.19
  111.3 13.2 copy-start.18
  111.3 13.3 copy-start.17
  230.7 2.0 copy-start.9
  236.8 1.0 copy-start.11
  388.5 49.0 %copy-start.2 = (f32[512,512]{1,0:T(8,128)}, f32[512,512]{1,0:T(8,128)S(1)}, u32[]{:S(2)}) copy-start(f32[512,512]{1,0:T(8,128)S(1)} %fusion.16) | copy-start | bytes 3145732
  444.7 1.0 copy-start.10
  585.9 93.8 %copy-start.4 = (f32[128,512]{1,0:T(8,128)}, f32[128,512]{1,0:T(8,128)S(1)}, u32[]{:S(2)}) copy-start(f32[128,512]{1,0:T(8,128)S(1)} %fusion.47) | copy-start | bytes 786436
  587.6 92.1 %copy-start.7 = (f32[128,512]{1,0:T(8,128)}, f32[128,512]{1,0:T(8,128)S(1)}, u32[]{:S(2)}) copy-start(f32[128,512]{1,0:T(8,128)S(1)} %fusion.70) | copy-start | bytes 786436
  589.5 1.7 copy-start.12
  821.9 140.0 %copy-start.6 = (f32[512,512]{1,0:T(8,128)S(1)}, f32[512,512]{1,0:T(8,128)}, u32[]{:S(2)}) copy-start(f32[512,512]{1,0:T(8,128)} %pad_maximum_fusion.4.clone.5) | copy-start | bytes 3145732
  1077.0 64.4 %copy-start.3 = (f32[512,512]{1,0:T(8,128)S(1)}, f32[512,512]{1,0:T(8,128)}, u32[]{:S(2)}) copy-start(f32[512,512]{1,0:T(8,128)} %copy-done.2) | copy-start | bytes 3145732
  1141.4 113.7 %copy-start.5 = (f32[128,512]{1,0:T(8,128)S(1)}, f32[128,512]{1,0:T(8,128)}, u32[]{:S(2)}) copy-start(f32[128,512]{1,0:T(8,128)} %copy-done.4) | copy-start | bytes 786436
  1141.4 113.7 %copy-start.8 = (f32[128,512]{1,0:T(8,128)S(1)}, f32[128,512]{1,0:T(8,128)}, u32[]{:S(2)}) copy-start(f32[128,512]{1,0:T(8,128)} %copy-done.7) | copy-start | bytes 786436
  1141.4 113.7 %copy-start.13 = (f32[128,512]{1,0:T(8,128)S(1)}, f32[128,512]{1,0:T(8,128)}, u32[]{:S(2)}) copy-start(f32[128,512]{1,0:T(8,128)} %copy-done.12) | copy-start | bytes 786436
  1141.4 113.7 %copy-start.14 = (f32[128,512]{1,0:T(8,128)S(1)}, f32[128,512]{1,0:T(8,128)}, u32[]{:S(2)}) copy-start(f32[128,512]{1,0:T(8,128)} %fusion.67) | copy-start | bytes 786436
  1435.2 78.3 %copy-start.1 = (bf16[1,180,1440]{2,1,0:T(8,128)(2,1)S(1)}, bf16[1,180,1440]{2,1,0:T(8,128)(2,1)}, u32[]{:S(2)}) copy-start(bf16[1,180,1440]{2,1,0:T(8,128)(2,1)} %param.7) | copy-start | bytes 1555204
Sparse Core Ops, SparseCore 0:
  106.3 52.5 all-reduce.4
where the time goes:
time: 1540 us; the launch traced here: 1520 us
  other arithmetic  495 us (32%)
  local copies, waits for them, and re-layouts  462 us (30%)
  matrix products  441 us (29%)
  waiting for transfers between devices  47.8 us (3%)
  blocking collectives  47 us (3%)
  between operations  20.1 us (1%)
    unnamed x5, other arithmetic  151 us
    scatter-add x1, local copies, waits for them, and re-layouts, on_device(): cov.at[row_pick, column_ids].add(jnp.where(inside, nug_rows[row_pick], 0.0))  140 us
    concatenate x2, local copies, waits for them, and re-layouts, on_device(): joined = jnp.concatenate([first, second], axis=1).astype(jnp.bfloat16)  129 us
    dot_general x1, matrix products, on_device(): second = jnp.dot(rest, inv22.T, precision=HIGH)  116 us
    dot_general x1, matrix products, on_device(): first = jnp.dot(cov[:, :panel], inv11.T, precision=HIGH)  115 us
    dot_general x1, matrix products, on_device(): rest = cov[:, panel:] - jnp.dot(first, l21.T, precision=HIGH)  114 us
    unnamed x47, local copies, waits for them, and re-layouts  103 us
    another operation x15, other arithmetic, on_device(): l11 = jnp.linalg.cholesky(block[:panel, :panel])  79.7 us
  transfers between devices with their start and end apart: 2, of which 2 were waited for; matrix products, arithmetic and copies ran while one was open for 1% of the time, Pallas kernels for 0%

commit v1 on v0

v1 whole, which is shorter than its diff:
```python
import functools
import math

import jax
import jax.numpy as jnp
import numpy as np
from jax import lax
from jax.experimental import pallas as pl
from jax.experimental.pallas import tpu as pltpu
from jax.sharding import PartitionSpec as P

LANE = 128
GROUP = 16
VMEM = 48 << 20
F32, BF16 = jnp.float32, jnp.bfloat16
NT = (((1,), (1,)), ((), ()))


def div_up(a, b):
    return -(-a // b)


def divisor(n, most):
    return max(d for d in range(1, most + 1) if n % d == 0)


def whole(a):
    return pl.BlockSpec(a.shape, lambda i, *_: (0,) * a.ndim)


def turn(r, n):
    x = (r - jnp.floor(r * (1.0 / n)) * n) * (4.0 / n)
    k = jnp.floor(x + 0.5)
    y = (x - k) * (math.pi / 2)
    z = y * y
    s = y * (1 + z * (-1 / 6 + z * (1 / 120 + z * (-1 / 5040 + z * (1 / 362880)))))
    c = 1 + z * (-1 / 2 + z * (1 / 24 + z * (-1 / 720 + z * (1 / 40320 - z * (1 / 3628800)))))
    odd = (k == 1) | (k == 3)
    cos = jnp.where(odd, s, c)
    sin = jnp.where(odd, c, s)
    cos = jnp.where((k == 1) | (k == 2), -cos, cos)
    sin = jnp.where((k == 2) | (k == 3), -sin, sin)
    return cos, sin


def spectra_kernel(n_lon, ords, rows, f_ref, o_ref, c_ref, s_ref):
    dest = pl.program_id(0)
    lats = f_ref.shape[0]
    tiles = rows // 8
    lane = lax.broadcasted_iota(jnp.int32, (tiles, 2 * LANE), 1)
    lane = jnp.where(lane < LANE, lane, LANE).astype(F32)
    first = (dest * ords + 8 * lax.broadcasted_iota(jnp.int32, (tiles, 2 * LANE), 0)).astype(F32)
    pc, ps = turn(first * lane, n_lon)
    few = lax.broadcasted_iota(jnp.int32, (8, 2 * LANE), 0).astype(F32)
    qc, qs = turn(few * lane[:1], n_lon)
    scale = 1.0 / math.sqrt(n_lon)
    for p in range(0, tiles, 2):
        both_c, both_s = [], []
        for i in (p, p + 1):
            both_c.append(pc[i : i + 1] * qc - ps[i : i + 1] * qs)
            both_s.append(ps[i : i + 1] * qc + pc[i : i + 1] * qs)
        cos = jnp.concatenate(both_c, axis=0)
        sin = jnp.concatenate(both_s, axis=0)
        rc, rs = cos[:, LANE:], sin[:, LANE:]
        c, s = cos[:, :LANE] * scale, sin[:, :LANE] * scale
        for a in range(div_up(n_lon, LANE)):
            width = min(LANE, n_lon - a * LANE)
            at = (slice(8 * p, 8 * p + 16), slice(a * LANE, a * LANE + width))
            c_ref[at] = c[:, :width].astype(BF16)
            s_ref[at] = (-s[:, :width]).astype(BF16)
            c, s = c * rc - s * rs, s * rc + c * rs
    f = f_ref[...]
    re = lax.dot_general(c_ref[...], f, NT, preferred_element_type=F32)
    im = lax.dot_general(s_ref[...], f, NT, preferred_element_type=F32)
    pad = jnp.zeros((rows, o_ref.shape[2] - 2 * lats), F32)
    o_ref[0] = jnp.concatenate([re, im, pad], axis=1).astype(BF16)


def spectra(fields, ords, dests):
    lats, n_lon = fields.shape
    rows = div_up(ords, GROUP) * GROUP
    lanes = div_up(2 * lats, LANE) * LANE
    return pl.pallas_call(
        functools.partial(spectra_kernel, n_lon, ords, rows),
        grid=(dests,),
        in_specs=[pl.BlockSpec((lats, n_lon), lambda i: (0, 0))],
        out_specs=pl.BlockSpec((1, rows, lanes), lambda i: (i, 0, 0)),
        out_shape=jax.ShapeDtypeStruct((dests, rows, lanes), BF16),
        scratch_shapes=[pltpu.VMEM((rows, n_lon), BF16), pltpu.VMEM((rows, n_lon), BF16)],
        compiler_params=pltpu.CompilerParams(vmem_limit_bytes=VMEM),
        name="spectra",
    )(fields)


def partial_kernel(
    dims, key_ref, keyn_ref, meta_ref, x_ref, leg_ref, nug_ref, perm_ref, sel_ref,
    keep_ref, send_ref, pick_ref, flat, turned, held, nugs,
):
    times, lats, ords, degs, blocks, deg_local, cols = dims
    step = pl.program_id(0)
    steps = pl.num_programs(0)
    width = 2 * times
    lanes = GROUP * width
    me, ord_start = meta_ref[0], meta_ref[1]

    @pl.when(step == 0)
    def _():
        held[...] = jnp.zeros_like(held)
        nugs[...] = jnp.zeros_like(nugs)

    x = x_ref[...].reshape(times * GROUP, x_ref.shape[2])
    x = jnp.dot(perm_ref[...], x, preferred_element_type=F32)
    re = x[:, :lats]
    im = x[:, lats : 2 * lats]
    deg = lax.broadcasted_iota(jnp.int32, (width, degs), 1)
    for r in range(GROUP):
        at = slice(times * r, times * r + times)
        row = jnp.concatenate([re[at], im[at]], axis=0).astype(BF16)
        y = jnp.dot(row, leg_ref[r], preferred_element_type=F32)
        order = step * GROUP + r
        least = jnp.where(order < ords, ord_start + order, degs)
        y = jnp.where(deg >= least, y, 0.0).astype(BF16).astype(F32)
        flat[width * r : width * (r + 1), :degs] = y
    turned[...] = flat[...].T
    for d in range(blocks):
        part = turned[deg_local * d : deg_local * (d + 1), :].astype(BF16)
        where = d ^ me

        @pl.when(where % 2 == 0)
        def _():
            keep_ref[where // 2] = part

        @pl.when(where % 2 == 1)
        def _():
            send_ref[where // 2] = part

    lane = lax.broadcasted_iota(jnp.int32, (1, lanes), 1)

    def pick(e, _):
        key = key_ref[e]
        k = key % cols
        place = key // cols
        c = place % 2
        l = place // 2 % degs
        m = place // (2 * degs) - step * GROUP
        low = (2 * m + c) * times
        row = turned[pl.ds(l, 1), :]
        held[pl.ds(k, 1), :] = jnp.where((lane >= low) & (lane < low + times), row, 0.0)
        return 0

    lax.fori_loop(meta_ref[3 + step], meta_ref[4 + step], pick, 0)

    @pl.when(step == steps - 1)
    def _():
        ords_lane = lax.broadcasted_iota(jnp.int32, (1, ords), 1)

        def pick_nugget(e, _):
            key = keyn_ref[e]
            k = key % cols
            place = key // cols
            c = place % 2
            m = place // 2 % ords
            row = nug_ref[place // (2 * ords), pl.ds(c, 1), :]
            nugs[pl.ds(k, 1), :ords] = jnp.where(ords_lane == m, row, 0.0)
            return 0

        lax.fori_loop(0, meta_ref[2], pick_nugget, 0)
        ones = jnp.ones((8, LANE), F32)
        for t in range(cols // LANE):
            at = slice(LANE * t, LANE * (t + 1))
            pick_ref[:times, t, :] = lax.dot_general(
                sel_ref[...], held[at, :].astype(BF16), NT, preferred_element_type=F32
            )
            got = lax.dot_general(
                ones, nugs[at, :], NT, preferred_element_type=F32, precision=lax.Precision.HIGHEST
            )
            pick_ref[times, pl.ds(t, 1), :] = got[:1]


def partials(moved, legendre, nugget, key, keyn, meta, blocks, cols):
    times, rows, width = moved.shape
    ords, lats, degs = legendre.shape
    deg_local = nugget.shape[0]
    lanes = GROUP * 2 * times
    steps = rows // GROUP
    n = times * GROUP
    perm = np.zeros((GROUP, times, times, GROUP), np.float32)
    for t in range(times):
        for m in range(GROUP):
            perm[m, t, t, m] = 1
    perm = jnp.asarray(perm.reshape(n, n), BF16)
    sel = jnp.asarray(np.tile(np.eye(times, dtype=np.float32), (1, 2 * GROUP)), BF16)
    half = jax.ShapeDtypeStruct((blocks // 2, deg_local, steps * lanes), BF16)
    half_spec = pl.BlockSpec((blocks // 2, deg_local, lanes), lambda i, *_: (0, 0, i))
    dims = (times, lats, ords, degs, blocks, deg_local, cols)
    assert ords <= LANE
    return pl.pallas_call(
        functools.partial(partial_kernel, dims),
        grid_spec=pltpu.PrefetchScalarGridSpec(
            num_scalar_prefetch=3,
            grid=(steps,),
            in_specs=[
                pl.BlockSpec((times, GROUP, width), lambda i, *_: (0, i, 0)),
                pl.BlockSpec((GROUP, lats, degs), lambda i, *_: (i, 0, 0)),
                whole(nugget),
                whole(perm),
                whole(sel),
            ],
            out_specs=[
                half_spec,
                half_spec,
                pl.BlockSpec((times + 1, cols // LANE, LANE), lambda i, *_: (0, 0, 0)),
            ],
            scratch_shapes=[
                pltpu.VMEM((lanes, div_up(degs, LANE) * LANE), F32),
                pltpu.VMEM((div_up(degs, LANE) * LANE, lanes), F32),
                pltpu.VMEM((cols, lanes), F32),
                pltpu.VMEM((cols, LANE), F32),
            ],
        ),
        out_shape=[half, half, jax.ShapeDtypeStruct((times + 1, cols // LANE, LANE), F32)],
        compiler_params=pltpu.CompilerParams(vmem_limit_bytes=VMEM),
        name="partials",
    )(key, keyn, meta, moved, legendre, nugget, perm, sel)


def factor_kernel(times, pick_ref, tri_ref, w_ref, ld_ref, held):
    tiles = pick_ref.shape[1]
    root = 1.0 / math.sqrt(times)
    u = [pick_ref[x].astype(BF16).astype(F32) * root for x in range(times)]
    nug = pick_ref[times]
    inv = 1.0 / nug
    un = [a * inv for a in u]
    pairs = [(a, b) for a in range(times) for b in range(a, times)]
    prod = jnp.concatenate([un[a] * u[b] for a, b in pairs], axis=0)
    sums = jnp.zeros((prod.shape[0], 2 * LANE), F32)
    for _ in range(3):
        part = prod.astype(BF16)
        sums = sums + jnp.dot(part, tri_ref[...], preferred_element_type=F32)
        prod = prod - part.astype(F32)
    row = lax.broadcasted_iota(jnp.int32, (tiles, LANE), 0)

    def shifted(v, by):
        return jnp.where(row >= by, pltpu.roll(v, by, axis=0), 0.0)

    g = {}
    for i, (a, b) in enumerate(pairs):
        at = slice(tiles * i, tiles * (i + 1))
        before = shifted(sums[at, LANE:], 1)
        by = 1
        while by < tiles:
            before = before + shifted(before, by)
            by *= 2
        g[a, b] = sums[at, :LANE] + before + (1.0 if a == b else 0.0)
    z = list(u)
    quad = jnp.zeros_like(nug)
    scaled = []
    for p in range(times):
        d = 1.0 / g[p, p]
        f = {a: g[p, a] * d for a in range(p + 1, times)}
        for a in range(p + 1, times):
            for b in range(a, times):
                g[a, b] = g[a, b] - f[a] * g[p, b]
            z[a] = z[a] - f[a] * z[p]
        quad = quad + z[p] * z[p] * d
        scaled.append((d, f))
    y = [None] * times
    for p in reversed(range(times)):
        d, f = scaled[p]
        y[p] = z[p] * d
        for b in range(p + 1, times):
            y[p] = y[p] - f[b] * y[b]
    diag = jnp.sqrt(nug + quad)
    over = root / diag
    for x in range(times):
        held[x] = y[x] * over
    zero = jnp.zeros((times, LANE), F32)
    for t in range(tiles):
        w = held[:, t, :]
        left = jnp.concatenate([w, zero], axis=1)
        right = jnp.concatenate([zero, w], axis=1)
        w_ref[4 * times * t : 4 * times * (t + 1)] = jnp.concatenate([left, left, right, right], axis=0).astype(BF16)
        ld_ref[2 * t : 2 * t + 2] = jnp.broadcast_to(diag[t : t + 1], (2, LANE))


def factor(picks):
    times, tiles = picks.shape[0] - 1, picks.shape[1]
    assert times % 8 == 0 and tiles == 8
    strict = np.triu(np.ones((LANE, LANE), np.float32), 1)
    tri = jnp.asarray(np.concatenate([strict, np.ones((LANE, LANE), np.float32)], axis=1), BF16)
    return pl.pallas_call(
        functools.partial(factor_kernel, times),
        out_shape=[
            jax.ShapeDtypeStruct((4 * times * tiles, 2 * LANE), BF16),
            jax.ShapeDtypeStruct((2 * tiles, LANE), F32),
        ],
        scratch_shapes=[pltpu.VMEM((times, tiles, LANE), F32)],
        compiler_params=pltpu.CompilerParams(vmem_limit_bytes=VMEM),
        name="factor",
    )(picks, tri)


def panel_kernel(dims, n_parts, key_ref, start_ref, *refs):
    times, ords, deg_local, block, inner = dims
    parts, (spread_ref, mask_ref, w_ref, ld_ref, o_ref, held) = refs[:n_parts], refs[n_parts:]
    step = pl.program_id(0)
    quads = div_up(ords, 2)
    per = LANE // (4 * times)
    kk = w_ref.shape[0]
    rows = mask_ref.shape[0]
    cols = rows // 2 * LANE

    @pl.when(step == 0)
    def _():
        total = sum(p[0].astype(F32) for p in parts).astype(BF16)
        for q in range(quads):
            w, s = divmod(q, per)
            held[q] = jnp.dot(
                total[:, LANE * w : LANE * (w + 1)],
                spread_ref[:, kk * s : kk * (s + 1)],
                preferred_element_type=F32,
            )

    mask = mask_ref[...]
    weights = w_ref[...]

    def some(i, _):
        lhs = []
        for u in range(inner):
            for q in range(quads):
                row = held[q, pl.ds(step * block + i * inner + u, 1), :]
                lhs.append(jnp.broadcast_to(row, (rows, kk)).astype(BF16) * mask)
        for at in range(0, len(lhs), 2 * quads):
            y = jnp.dot(
                jnp.concatenate(lhs[at : at + 2 * quads], axis=0), weights, preferred_element_type=F32
            ).astype(BF16)
            for j in range(at, min(at + 2 * quads, len(lhs))):
                u, q = divmod(j, quads)
                for h in range(2):
                    if 2 * q + h < ords:
                        o_ref[i * inner + u, 2 * q + h] = y[
                            rows * (j - at) : rows * (j - at + 1), LANE * h : LANE * (h + 1)
                        ]
        return 0

    lax.fori_loop(0, block // inner, some, 0)

    index = lax.broadcasted_iota(jnp.int32, (rows, LANE), 0)
    col = index // 2 * LANE + lax.broadcasted_iota(jnp.int32, (rows, LANE), 1)

    def chosen_row(e, _):
        key = key_ref[e]
        k = key % cols
        place = key // cols
        c = place % 2
        m = place // 2 % ords
        l = place // (2 * ords) - step * block
        old = o_ref[l, m].astype(F32)
        new = jnp.where(col < k, old, jnp.where(col == k, ld_ref[...], 0.0))
        o_ref[l, m] = jnp.where(index % 2 == c, new, old).astype(BF16)
        return 0

    lax.fori_loop(start_ref[step], start_ref[step + 1], chosen_row, 0)


def panels(key, starts, parts, weights, diag, dims):
    times, ords, deg_local, block, inner = dims
    quads = div_up(ords, 2)
    kk = weights.shape[0]
    rows = diag.shape[0]
    width = 4 * times
    lane = np.arange(LANE)[:, None]
    col = np.arange(LANE // width * kk)[None, :]
    spread = jnp.asarray(lane == col // kk * width + col % width, BF16)
    r = np.arange(rows)[:, None]
    z = np.arange(kk)[None, :]
    mask = jnp.asarray((r // 2 == z // width) & (r % 2 == z // times % 2), BF16)
    part_spec = pl.BlockSpec((1,) + parts[0].shape[1:], lambda i, *_: (0, 0, 0))
    out = pl.pallas_call(
        functools.partial(panel_kernel, dims, len(parts)),
        grid_spec=pltpu.PrefetchScalarGridSpec(
            num_scalar_prefetch=2,
            grid=(deg_local // block,),
            in_specs=[part_spec] * len(parts) + [whole(a) for a in (spread, mask, weights, diag)],
            out_specs=pl.BlockSpec((block, ords, rows, LANE), lambda i, *_: (i, 0, 0, 0)),
            scratch_shapes=[pltpu.VMEM((quads, deg_local, kk), F32)],
        ),
        out_shape=jax.ShapeDtypeStruct((deg_local, ords, rows, LANE), BF16),
        compiler_params=pltpu.CompilerParams(vmem_limit_bytes=VMEM),
        name="panels",
    )(key, starts, *parts, spread, mask, weights, diag)
    out = out.reshape(deg_local, ords, rows // 2, 2, LANE)
    return jnp.transpose(out, (0, 1, 3, 2, 4)).reshape(deg_local, ords, 2, rows // 2 * LANE)


def partner(axis, bit):
    size = lax.axis_size(axis)
    return [(i, i ^ bit) for i in range(size)]


def bits(axis):
    size = lax.axis_size(axis)
    return [1 << s for s in range(size.bit_length() - 1)]


def on_device(fields, legendre, nugget, chosen):
    ords, degs = legendre.shape[1], legendre.shape[2]
    deg_local = nugget.shape[0]
    tm, lat = lax.axis_size("tm"), lax.axis_size("lat")
    cols = chosen.shape[0]
    block = divisor(deg_local, 12)
    inner = divisor(block, 6)
    me = lax.axis_index("lat")
    ord_start = lax.axis_index("tm") * ords
    deg_start = me * deg_local

    sent = spectra(fields.reshape(-1, fields.shape[-1]), ords, tm)

    k = jnp.arange(cols, dtype=jnp.int32)
    deg = chosen // (2 * tm * ords)
    order = chosen // 2 % (tm * ords) - ord_start
    part = chosen % 2
    mine = (order >= 0) & (order < ords)
    here = mine & (deg >= deg_start) & (deg < deg_start + deg_local)
    none = jnp.int32(2**31 - 1)
    key = jnp.where(mine, ((order * degs + deg) * 2 + part) * cols + k, none)
    keyn = jnp.where(here, (((deg - deg_start) * ords + order) * 2 + part) * cols + k, none)
    both = jnp.sort(jnp.stack([key, keyn]), axis=1)
    steps = div_up(ords, GROUP)
    edge = jnp.arange(steps + 1, dtype=jnp.int32) * (GROUP * degs * 2 * cols)
    edge = edge.at[steps].set(none)
    groups = jnp.sum((key[None, :] < edge[:, None]).astype(jnp.int32), axis=1)
    edge = jnp.arange(deg_local // block + 1, dtype=jnp.int32) * (block * ords * 2 * cols)
    starts = jnp.sum((keyn[None, :] < edge[:, None]).astype(jnp.int32), axis=1)
    meta = jnp.concatenate([jnp.stack([me, ord_start, starts[-1]]).astype(jnp.int32), groups])

    moved = lax.all_to_all(sent, "tm", split_axis=0, concat_axis=0, tiled=True)
    keep, send, picks = partials(
        moved, jnp.transpose(legendre, (1, 0, 2)), jnp.transpose(nugget, (0, 2, 1)),
        both[0], both[1], meta, lat, cols,
    )
    times = moved.shape[0]
    parts = [keep, lax.ppermute(send, "lat", partner("lat", 1))]
    for bit in bits("lat")[1:]:
        out = sum(p[1::2].astype(F32) for p in parts).astype(BF16)
        parts = [p[0::2] if p.shape[0] > 2 else p for p in parts]
        parts.append(lax.ppermute(out, "lat", partner("lat", bit)))
    for axis in ("lat", "tm"):
        for bit in bits(axis):
            picks = picks + lax.ppermute(picks, axis, partner(axis, bit))
    weights, diag = factor(picks)
    return panels(both[1], starts, parts, weights, diag, (times, ords, deg_local, block, inner))


def solution(mesh):
    placed = (P("tm", "lat", None), P("lat", "tm", None), P("lat", "tm", None), P())
    return jax.shard_map(
        on_device, mesh=mesh, in_specs=placed, out_specs=P("lat", "tm", None, None), check_vma=False
    )
```

time: 1540 us -> 129 us (0.08); the launches traced: 1520 us -> 129 us
  other arithmetic: 495 us -> 1.96 us
  local copies, waits for them, and re-layouts: 462 us -> 9.7 us
  matrix products: 441 us -> 0 us
  Pallas kernels: 0 us -> 58.5 us
  blocking collectives: 47 us -> 0 us
    dot_general x9 -> x0, matrix products: 417 us -> none  [the longest x1 116 us: on_device(): second = jnp.dot(rest, inv22.T, precision=HIGH)]
    another operation x38 -> x1, other arithmetic: 263 us -> 0.61 us  [on_device(): both = jnp.sort(jnp.stack([key, keyn]), axis=1)]
    unnamed x5 -> x0, other arithmetic: 151 us -> none
    scatter-add x1 -> x0, local copies, waits for them, and re-layouts: 140 us -> none  [on_device(): cov.at[row_pick, column_ids].add(jnp.where(inside, nug_rows[row_pick], 0.0))]
    concatenate x2 -> x0, local copies, waits for them, and re-layouts: 129 us -> none  [on_device(): joined = jnp.concatenate([first, second], axis=1).astype(jnp.bfloat16)]
    unnamed x47 -> x17, local copies, waits for them, and re-layouts: 103 us -> 1.11 us
    concatenate x1, other arithmetic: 78.3 us -> 0.77 us  [on_device(): jnp.concatenate([jnp.stack([me, ord_start, starts[-1]]).astype(jnp.int32)...]
    pallas_call x0 -> x4, Pallas kernels: none -> 58.5 us  [the longest x1 31.3 us: panels(): pl.pallas_call(functools.partial(panel_kernel, dims, len(parts)), grid_sp...]
  transfers between devices with their start and end apart: 2 -> 8, of which waited for: 2 -> 7; matrix products, arithmetic and copies ran while one was open for 1% -> 3% of each run, Pallas kernels for 0% -> 0%
where the time goes in v1:
time: 129 us
  Pallas kernels  58.5 us (45%)
  waiting for transfers between devices  35.4 us (27%)
  between operations  13.6 us (11%)
  starting transfers between devices  9.78 us (8%)
  local copies, waits for them, and re-layouts  9.7 us (8%)
  other arithmetic  1.96 us (2%)
    pallas_call x1, Pallas kernels, panels(): pl.pallas_call(functools.partial(panel_kernel, dims, len(parts)), grid_sp...  31.3 us
    ppermute x5, waiting for transfers between devices, on_device(): picks = picks + lax.ppermute(picks, axis, partner(axis, bit))  26.3 us
    pallas_call x1, Pallas kernels, partials(): pl.pallas_call(functools.partial(partial_kernel, dims), grid_spec=pltpu.P...  21.3 us
    all_to_all x1, starting transfers between devices, on_device(): moved = lax.all_to_all(sent, 'tm', split_axis=0, concat_axis=0, tiled=True)  7.25 us
    all_to_all x1, waiting for transfers between devices, on_device(): moved = lax.all_to_all(sent, 'tm', split_axis=0, concat_axis=0, tiled=True)  6.41 us
    sort x2, local copies, waits for them, and re-layouts, on_device(): both = jnp.sort(jnp.stack([key, keyn]), axis=1)  6.16 us
    pallas_call x1, Pallas kernels, spectra(): pl.pallas_call(functools.partial(spectra_kernel, n_lon, ords, rows), grid...  5.58 us
    ppermute x1, waiting for transfers between devices, on_device(): parts = [keep, lax.ppermute(send, 'lat', partner('lat', 1))]  2.73 us
  transfers between devices with their start and end apart: 8, of which 7 were waited for; matrix products, arithmetic and copies ran while one was open for 3% of the time, Pallas kernels for 0%

profile of v1, /device:TPU:0, one launch (start us, length us, event | category | flops | bytes accessed | tf_op | source)
XLA Modules:
  0.0 128.9 jit_solution(2054940420521862861)
XLA Ops:
  6.5 1.1 copy-done
  7.6 5.6 %spectra.1 = bf16[8,96,384]{2,1,0:T(8,128)(2,1)} custom-call(bf16[180,1440]{1,0:T(8,128)(2,1)S(1)} %bitcast.14), custom_call_target="tpu_custom_call" | custom-call | tf_op jit(solution)/shard_map/spectra/pallas_call | solution.py:83
  13.2 7.3 %all-to-all-start = ((bf16[8,96,384]{2,1,0:T(8,128)(2,1)}), bf16[8,96,384]{2,1,0:T(8,128)(2,1)S(1)}, u32[]{:S(2)}, u32[]{:S(2)}) async-start(bf16[8,96,384]{2,1,0:T(8,128)(2,1)} %spectra.1), calls=%async_computation | async-start | bytes 1179648 | tf_op jit(solution)/shard_map/all_to_all | solution.py:437
  20.4 0.0 sort.10.cloned.1.call-start
  20.5 0.6 pad_add_fusion
  21.1 0.0 sort.10.cloned.1.call-update
  21.2 0.2 convert_reduce_fusion.start_ref
  21.4 0.7 slice.29
  22.1 0.2 convert_reduce_fusion.1
  22.2 0.8 pad_add_fusion.1.meta_ref
  23.0 6.1 %sort.10.cloned.1.call-done = s32[2,1024]{1,0:T(2,128)} async-done(((s32[2,1024]{1,0:T(2,128)}), s32[2,1024]{1,0:T(2,128)}) %sort.10.cloned.1.call-update) | async-done | bytes 8208 | tf_op jit(solution)/shard_map/jit(sort)/sort | solution.py:428
  29.1 0.8 fusion.4
  29.9 6.4 %all-to-all-done.x_ref = bf16[8,96,384]{2,1,0:T(8,128)(2,1)S(1)} async-done(((bf16[8,96,384]{2,1,0:T(8,128)(2,1)}), bf16[8,96,384]{2,1,0:T(8,128)(2,1)S(1)}, u32[]{:S(2)}, u32[]{:S(2)}) %all-to-all-start) | async-done | bytes 589856 | tf_op jit(solution)/shard_map/all_to_all | solution.py:437
  36.3 21.3 %partials.1 = (bf16[2,180,1536]{2,1,0:T(8,128)(2,1)S(1)}, bf16[2,180,1536]{2,1,0:T(8,128)(2,1)S(1)}, f32[9,8,128]{2,1,0:T(8,128)S(1)}) custom-call(s32[1024]{0:T(1024)S(1)} %bitcast.18, s32[1024]{0:T(1024)S(1)} %bitcast.16, s32[10]{0:T(128)S(1)} %pad_add_fusion.1.meta_ref, bf16[8,96,384]{2,1,0:T(8,128)(2,1)S(1)} %all-to-all-done.x_ref, ...), custom_call_target="tpu_custom_call" | custom-call | tf_op jit(solution)/shard_map/partials/pallas_call | solution.py:197
  57.6 0.9 copy.15
  58.5 0.1 collective-permute-start
  58.5 2.7 %collective-permute-done = bf16[2,180,1536]{2,0,1:T(2,128)(2,1)S(1)} collective-permute-done((bf16[2,180,1536]{2,0,1:T(2,128)(2,1)S(1)}, bf16[2,180,1536]{2,0,1:T(2,128)(2,1)S(1)}, u32[]{:S(2)}, u32[]{:S(2)}) %collective-permute-start) | collective-permute-done | bytes 1105952 | tf_op jit(solution)/shard_map/ppermute | solution.py:443
  61.3 0.1 copy.17.refs_1_
  61.4 0.0 copy-start.3
  61.4 0.0 copy-start.1
  61.4 0.0 copy-start.5
  61.4 0.1 add_convert_fusion
  61.6 2.1 %collective-permute-start.1 = (bf16[1,180,1536]{2,1,0:T(8,128)(2,1)S(1)}, bf16[1,180,1536]{2,1,0:T(8,128)(2,1)S(1)}, u32[]{:S(2)}, u32[]{:S(2)}) collective-permute-start(bf16[1,180,1536]{2,1,0:T(8,128)(2,1)S(1)} %add_convert_fusion), channel_id=1, source_target_pairs={{0,2},{1,3},{2,0},{3,1},{4,6},{5,7},{6,4},{7,5},{8,10},{9,11},{10,... | collective-permute-start | bytes 1658888 | tf_op jit(solution)/shard_map/ppermute | solution.py:447
  63.6 1.2 collective-permute-done.2
  64.9 0.1 collective-permute-start.3
  64.9 12.6 %collective-permute-done.3 = f32[9,8,128]{2,1,0:T(8,128)S(1)} collective-permute-done((f32[9,8,128]{2,1,0:T(8,128)S(1)}, f32[9,8,128]{2,1,0:T(8,128)S(1)}, u32[]{:S(2)}, u32[]{:S(2)}) %collective-permute-start.3) | collective-permute-done | bytes 36896 | tf_op jit(solution)/shard_map/ppermute | solution.py:450
  77.5 0.3 collective-permute-start.4
  77.8 3.7 %collective-permute-done.4 = f32[9,8,128]{2,1,0:T(8,128)S(1)} collective-permute-done((f32[9,8,128]{2,1,0:T(8,128)S(1)}, f32[9,8,128]{2,1,0:T(8,128)S(1)}, u32[]{:S(2)}, u32[]{:S(2)}) %collective-permute-start.4) | collective-permute-done | bytes 36896 | tf_op jit(solution)/shard_map/ppermute | solution.py:450
  81.5 3.9 %collective-permute-done.5 = f32[9,8,128]{2,1,0:T(8,128)S(1)} collective-permute-done((f32[9,8,128]{2,1,0:T(8,128)S(1)}, f32[9,8,128]{2,1,0:T(8,128)S(1)}, u32[]{:S(2)}, u32[]{:S(2)}) %collective-permute-start.5) | collective-permute-done | bytes 36896 | tf_op jit(solution)/shard_map/ppermute | solution.py:450
  85.5 4.8 %collective-permute-done.6 = f32[9,8,128]{2,1,0:T(8,128)S(1)} collective-permute-done((f32[9,8,128]{2,1,0:T(8,128)S(1)}, f32[9,8,128]{2,1,0:T(8,128)S(1)}, u32[]{:S(2)}, u32[]{:S(2)}) %collective-permute-start.6) | collective-permute-done | bytes 36896 | tf_op jit(solution)/shard_map/ppermute | solution.py:450
  90.3 0.4 factor.1
  90.8 31.3 %panels.1 = bf16[180,90,16,128]{3,2,1,0:T(8,128)(2,1)} custom-call(s32[1024]{0:T(1024)S(1)} %bitcast.17, s32[16]{0:T(128)S(1)} %convert_reduce_fusion.start_ref, bf16[2,180,1536]{2,1,0:T(8,128)(2,1)S(1)} %get-tuple-element.22.refs_0_, bf16[2,180,1536]{2,1,0:T(8,128)(2,1)S(1)} %copy.17.refs_1_, bf16[1,180,1536]{2,1,0:T(8,128)(2,1)S(1)} %collective-permute-done.1.refs_2_, ...), custom_call_target="tpu_custom_call" | custom-call | tf_op jit(solution)/shard_map/panels/pallas_call | solution.py:379
  (25 shorter events, 0.1 us)
Async XLA Ops:
  6.5 1.1 copy-start
  7.6 12.9 %copy-start.7 = (s32[1024]{0:T(1024)S(1)}, s32[1024]{0:T(1024)}, u32[]{:S(2)}) copy-start(s32[1024]{0:T(1024)} %param.14) | copy-start | bytes 12292
  7.6 28.7 %copy-start.2 = (f32[180,90,2]{1,2,0:T(2,128)S(1)}, f32[180,90,2]{1,2,0:T(2,128)}, u32[]{:S(2)}) copy-start(f32[180,90,2]{1,2,0:T(2,128)} %param.13) | copy-start | bytes 388804
  7.6 28.7 %copy-start.4 = (bf16[128,128]{1,0:T(8,128)(2,1)S(1)}, bf16[128,128]{1,0:T(8,128)(2,1)}, u32[]{:S(2)}) copy-start(bf16[128,128]{1,0:T(8,128)(2,1)} %constant.109.clone.perm_ref) | copy-start | bytes 98308
  7.6 28.7 %copy-start.6 = (bf16[8,256]{1,0:T(8,128)(2,1)S(1)}, bf16[8,256]{1,0:T(8,128)(2,1)}, u32[]{:S(2)}) copy-start(bf16[8,256]{1,0:T(8,128)(2,1)} %constant.110.clone.sel_ref) | copy-start | bytes 12292
  13.2 23.1 %all-to-all-start = ((bf16[8,96,384]{2,1,0:T(8,128)(2,1)}), bf16[8,96,384]{2,1,0:T(8,128)(2,1)S(1)}, u32[]{:S(2)}, u32[]{:S(2)}) async-start(bf16[8,96,384]{2,1,0:T(8,128)(2,1)} %spectra.1), calls=%async_computation | async-start | bytes 1179648 | tf_op jit(solution)/shard_map/all_to_all | solution.py:437
  20.4 8.7 %sort.10.cloned.1.call-start = ((), (), s32[]{:S(2)}) async-start(), calls=%async_computation.1 | async-start | bytes 24608 | tf_op jit(solution)/shard_map/jit(sort)/sort | solution.py:428
  58.5 2.8 %collective-permute-start = (bf16[2,180,1536]{2,0,1:T(2,128)(2,1)S(1)}, bf16[2,180,1536]{2,0,1:T(2,128)(2,1)S(1)}, u32[]{:S(2)}, u32[]{:S(2)}) collective-permute-start(bf16[2,180,1536]{2,0,1:T(2,128)(2,1)S(1)} %copy.15), channel_id=1, source_target_pairs={{0,1},{1,0},{2,3},{3,2},{4,5},{5,4},{6,7},{7,6},{8,9},{9,8},{10,11... | collective-permute-start | bytes 3317768 | tf_op jit(solution)/shard_map/ppermute | solution.py:443
  61.4 29.0 %copy-start.3 = (bf16[128,256]{1,0:T(8,128)(2,1)S(1)}, bf16[128,256]{1,0:T(8,128)(2,1)}, u32[]{:S(2)}) copy-start(bf16[128,256]{1,0:T(8,128)(2,1)} %constant.111.clone.tri_ref) | copy-start | bytes 196612
  61.4 29.3 %copy-start.1 = (bf16[128,1024]{1,0:T(8,128)(2,1)S(1)}, bf16[128,1024]{1,0:T(8,128)(2,1)}, u32[]{:S(2)}) copy-start(bf16[128,1024]{1,0:T(8,128)(2,1)} %constant.112.clone.refs_3_) | copy-start | bytes 786436
  61.4 29.3 %copy-start.5 = (bf16[16,256]{1,0:T(8,128)(2,1)S(1)}, bf16[16,256]{1,0:T(8,128)(2,1)}, u32[]{:S(2)}) copy-start(bf16[16,256]{1,0:T(8,128)(2,1)} %constant.113.clone.refs_4_) | copy-start | bytes 24580
  61.6 29.2 %collective-permute-start.1 = (bf16[1,180,1536]{2,1,0:T(8,128)(2,1)S(1)}, bf16[1,180,1536]{2,1,0:T(8,128)(2,1)S(1)}, u32[]{:S(2)}, u32[]{:S(2)}) collective-permute-start(bf16[1,180,1536]{2,1,0:T(8,128)(2,1)S(1)} %add_convert_fusion), channel_id=1, source_target_pairs={{0,2},{1,3},{2,0},{3,1},{4,6},{5,7},{6,4},{7,5},{8,10},{9,11},{10,... | collective-permute-start | bytes 1658888 | tf_op jit(solution)/shard_map/ppermute | solution.py:447
  63.6 1.2 collective-permute-start.2
  64.9 12.7 %collective-permute-start.3 = (f32[9,8,128]{2,1,0:T(8,128)S(1)}, f32[9,8,128]{2,1,0:T(8,128)S(1)}, u32[]{:S(2)}, u32[]{:S(2)}) collective-permute-start(f32[9,8,128]{2,1,0:T(8,128)S(1)} %add.63), channel_id=1, source_target_pairs={{0,2},{1,3},{2,0},{3,1},{4,6},{5,7},{6,4},{7,5},{8,10},{9,11},{10,... | collective-permute-start | bytes 110600 | tf_op jit(solution)/shard_map/ppermute | solution.py:450
  77.5 4.0 %collective-permute-start.4 = (f32[9,8,128]{2,1,0:T(8,128)S(1)}, f32[9,8,128]{2,1,0:T(8,128)S(1)}, u32[]{:S(2)}, u32[]{:S(2)}) collective-permute-start(f32[9,8,128]{2,1,0:T(8,128)S(1)} %add.64), channel_id=1, source_target_pairs={{0,4},{4,0},{8,12},{12,8},{16,20},{20,16},{24,28},{28,24},{1,5},{5... | collective-permute-start | bytes 110600 | tf_op jit(solution)/shard_map/ppermute | solution.py:450
  81.5 4.0 %collective-permute-start.5 = (f32[9,8,128]{2,1,0:T(8,128)S(1)}, f32[9,8,128]{2,1,0:T(8,128)S(1)}, u32[]{:S(2)}, u32[]{:S(2)}) collective-permute-start(f32[9,8,128]{2,1,0:T(8,128)S(1)} %add.65), channel_id=1, source_target_pairs={{0,8},{4,12},{8,0},{12,4},{16,24},{20,28},{24,16},{28,20},{1,9},{5... | collective-permute-start | bytes 110600 | tf_op jit(solution)/shard_map/ppermute | solution.py:450
  85.5 4.9 %collective-permute-start.6 = (f32[9,8,128]{2,1,0:T(8,128)S(1)}, f32[9,8,128]{2,1,0:T(8,128)S(1)}, u32[]{:S(2)}, u32[]{:S(2)}) collective-permute-start(f32[9,8,128]{2,1,0:T(8,128)S(1)} %add.66), channel_id=1, source_target_pairs={{0,16},{4,20},{8,24},{12,28},{16,0},{20,4},{24,8},{28,12},{1,17},{... | collective-permute-start | bytes 110600 | tf_op jit(solution)/shard_map/ppermute | solution.py:450
Sparse Core Ops, SparseCore 0:
  23.7 5.1 sort.12.cloned.1.call-done
  (1 shorter events, 0.0 us)

commit v2 on v1

v2 whole, which is shorter than its diff:
```python
import functools
import math

import jax
import jax.numpy as jnp
import numpy as np
from jax import lax
from jax.experimental import pallas as pl
from jax.experimental.pallas import tpu as pltpu
from jax.sharding import PartitionSpec as P

LANE = 128
ROWS = 16
GROUP = 16
VMEM = 48 << 20
F32, BF16 = jnp.float32, jnp.bfloat16
NT = (((1,), (1,)), ((), ()))


def div_up(a, b):
    return -(-a // b)


def shifts(cols, minor):
    part = (cols - 1).bit_length()
    return part, part + 1, part + 1 + (minor - 1).bit_length()


def make_key(k, part, minor, major, cols, size):
    at = shifts(cols, size)
    return k | (part << at[0]) | (minor << at[1]) | (major << at[2])


def split_key(key, cols, size):
    at = shifts(cols, size)
    low = lambda x, n: x & ((1 << n) - 1)
    return low(key, at[0]), low(key >> at[0], 1), low(key >> at[1], at[2] - at[1]), key >> at[2]


def divisor(n, most):
    return max(d for d in range(1, most + 1) if n % d == 0)


def whole(a):
    return pl.BlockSpec(a.shape, lambda i, *_: (0,) * a.ndim)


def turn(r, n):
    x = (r - jnp.floor(r * (1.0 / n)) * n) * (4.0 / n)
    k = jnp.floor(x + 0.5)
    y = (x - k) * (math.pi / 2)
    z = y * y
    s = y * (1 + z * (-1 / 6 + z * (1 / 120 + z * (-1 / 5040 + z * (1 / 362880)))))
    c = 1 + z * (-1 / 2 + z * (1 / 24 + z * (-1 / 720 + z * (1 / 40320 - z * (1 / 3628800)))))
    odd = (k == 1) | (k == 3)
    cos = jnp.where(odd, s, c)
    sin = jnp.where(odd, c, s)
    cos = jnp.where((k == 1) | (k == 2), -cos, cos)
    sin = jnp.where((k == 2) | (k == 3), -sin, sin)
    return cos, sin


def spectra_kernel(n_lon, ords, rows, f_ref, o_ref, c_ref, s_ref):
    dest = pl.program_id(0)
    lats = f_ref.shape[0]
    tiles = rows // 8
    lane = lax.broadcasted_iota(jnp.int32, (tiles, 2 * LANE), 1)
    lane = jnp.where(lane < LANE, lane, LANE).astype(F32)
    first = (dest * ords + 8 * lax.broadcasted_iota(jnp.int32, (tiles, 2 * LANE), 0)).astype(F32)
    pc, ps = turn(first * lane, n_lon)
    few = lax.broadcasted_iota(jnp.int32, (8, 2 * LANE), 0).astype(F32)
    qc, qs = turn(few * lane[:1], n_lon)
    scale = 1.0 / math.sqrt(n_lon)
    for p in range(0, tiles, 2):
        both_c, both_s = [], []
        for i in (p, p + 1):
            both_c.append(pc[i : i + 1] * qc - ps[i : i + 1] * qs)
            both_s.append(ps[i : i + 1] * qc + pc[i : i + 1] * qs)
        cos = jnp.concatenate(both_c, axis=0)
        sin = jnp.concatenate(both_s, axis=0)
        rc, rs = cos[:, LANE:], sin[:, LANE:]
        c, s = cos[:, :LANE] * scale, sin[:, :LANE] * scale
        for a in range(div_up(n_lon, LANE)):
            width = min(LANE, n_lon - a * LANE)
            at = (slice(8 * p, 8 * p + 16), slice(a * LANE, a * LANE + width))
            c_ref[at] = c[:, :width].astype(BF16)
            s_ref[at] = (-s[:, :width]).astype(BF16)
            c, s = c * rc - s * rs, s * rc + c * rs
    f = f_ref[...]
    re = lax.dot_general(c_ref[...], f, NT, preferred_element_type=F32)
    im = lax.dot_general(s_ref[...], f, NT, preferred_element_type=F32)
    pad = jnp.zeros((rows, o_ref.shape[2] - 2 * lats), F32)
    o_ref[0] = jnp.concatenate([re, im, pad], axis=1).astype(BF16)


def spectra(fields, ords, dests):
    lats, n_lon = fields.shape
    rows = div_up(ords, GROUP) * GROUP
    lanes = div_up(2 * lats, LANE) * LANE
    return pl.pallas_call(
        functools.partial(spectra_kernel, n_lon, ords, rows),
        grid=(dests,),
        in_specs=[pl.BlockSpec((lats, n_lon), lambda i: (0, 0))],
        out_specs=pl.BlockSpec((1, rows, lanes), lambda i: (i, 0, 0)),
        out_shape=jax.ShapeDtypeStruct((dests, rows, lanes), BF16),
        scratch_shapes=[pltpu.VMEM((rows, n_lon), BF16), pltpu.VMEM((rows, n_lon), BF16)],
        compiler_params=pltpu.CompilerParams(vmem_limit_bytes=VMEM),
        name="spectra",
    )(fields)


def partial_kernel(
    dims, key_ref, meta_ref, x_ref, leg_ref, nug_ref, perm_ref, sel_ref,
    keep_ref, send_ref, pick_ref, flat, turned, held,
):
    times, lats, ords, degs, blocks, deg_local, cols = dims
    step = pl.program_id(0)
    steps = pl.num_programs(0)
    width = 2 * times
    lanes = GROUP * width
    me, ord_start = meta_ref[0], meta_ref[1]

    @pl.when(step == 0)
    def _():
        held[...] = jnp.zeros_like(held)

    x = x_ref[...].reshape(times * GROUP, x_ref.shape[2])
    x = jnp.dot(perm_ref[...], x, preferred_element_type=F32)
    re = x[:, :lats]
    im = x[:, lats : 2 * lats]
    deg = lax.broadcasted_iota(jnp.int32, (width, degs), 1)
    def order_rows(r):
        at = slice(times * r, times * r + times)
        row = jnp.concatenate([re[at], im[at]], axis=0).astype(BF16)
        y = jnp.dot(row, leg_ref[r], preferred_element_type=F32)
        least = ord_start + step * GROUP + r
        flat[width * r : width * (r + 1), :degs] = jnp.where(deg >= least, y, 0.0).astype(BF16).astype(F32)

    full = ords - (div_up(ords, GROUP) - 1) * GROUP
    for r in range(full):
        order_rows(r)

    @pl.when(step < steps - 1)
    def _():
        for r in range(full, GROUP):
            order_rows(r)

    turned[...] = flat[...].T
    for d in range(blocks):
        part = turned[deg_local * d : deg_local * (d + 1), :].astype(BF16)
        where = d ^ me

        @pl.when(where % 2 == 0)
        def _():
            keep_ref[where // 2] = part

        @pl.when(where % 2 == 1)
        def _():
            send_ref[where // 2] = part

    lane = lax.broadcasted_iota(jnp.int32, (1, lanes), 1)

    def pick(e, _):
        k, c, l, m = split_key(key_ref[e], cols, degs)
        low = (2 * (m - step * GROUP) + c) * times
        row = turned[pl.ds(l, 1), :]
        held[pl.ds(k, 1), :] = jnp.where((lane >= low) & (lane < low + times), row, 0.0)
        return 0

    lax.fori_loop(meta_ref[2 + step], meta_ref[3 + step], pick, 0)

    @pl.when(step == steps - 1)
    def _():
        for t in range(cols // LANE):
            at = slice(LANE * t, LANE * (t + 1))
            pick_ref[:times, t, :] = lax.dot_general(
                sel_ref[...], held[at, :].astype(BF16), NT, preferred_element_type=F32
            )
        pick_ref[times] = nug_ref[...]


def partials(moved, legendre, nuggets, key, meta, blocks, cols):
    times, rows, width = moved.shape
    ords, lats, degs = legendre.shape
    deg_local = degs // blocks
    lanes = GROUP * 2 * times
    steps = rows // GROUP
    n = times * GROUP
    perm = np.zeros((GROUP, times, times, GROUP), np.float32)
    for t in range(times):
        for m in range(GROUP):
            perm[m, t, t, m] = 1
    perm = jnp.asarray(perm.reshape(n, n), BF16)
    sel = jnp.asarray(np.tile(np.eye(times, dtype=np.float32), (1, 2 * GROUP)), BF16)
    half = jax.ShapeDtypeStruct((blocks // 2, deg_local, steps * lanes), BF16)
    half_spec = pl.BlockSpec((blocks // 2, deg_local, lanes), lambda i, *_: (0, 0, i))
    dims = (times, lats, ords, degs, blocks, deg_local, cols)
    return pl.pallas_call(
        functools.partial(partial_kernel, dims),
        grid_spec=pltpu.PrefetchScalarGridSpec(
            num_scalar_prefetch=2,
            grid=(steps,),
            in_specs=[
                pl.BlockSpec((times, GROUP, width), lambda i, *_: (0, i, 0)),
                pl.BlockSpec((GROUP, lats, degs), lambda i, *_: (i, 0, 0)),
                whole(nuggets),
                whole(perm),
                whole(sel),
            ],
            out_specs=[
                half_spec,
                half_spec,
                pl.BlockSpec((times + 1, cols // LANE, LANE), lambda i, *_: (0, 0, 0)),
            ],
            scratch_shapes=[
                pltpu.VMEM((lanes, div_up(degs, LANE) * LANE), F32),
                pltpu.VMEM((div_up(degs, LANE) * LANE, lanes), F32),
                pltpu.VMEM((cols, lanes), F32),
            ],
        ),
        out_shape=[half, half, jax.ShapeDtypeStruct((times + 1, cols // LANE, LANE), F32)],
        compiler_params=pltpu.CompilerParams(vmem_limit_bytes=VMEM),
        name="partials",
    )(key, meta, moved, legendre, nuggets, perm, sel)


def nugget_kernel(dims, key_ref, count_ref, nug_ref, o_ref, held):
    ords, cols = dims
    held[...] = jnp.zeros_like(held)
    order = lax.broadcasted_iota(jnp.int32, (1, ords), 1)

    def pick(e, _):
        k, c, m, l = split_key(key_ref[e], cols, ords)
        row = nug_ref[l, pl.ds(c, 1), :]
        held[pl.ds(k, 1), :ords] = jnp.where(order == m, row, 0.0)
        return 0

    lax.fori_loop(0, count_ref[0], pick, 0)
    for t in range(cols // LANE):
        got = lax.dot_general(
            jnp.ones((8, LANE), F32),
            held[LANE * t : LANE * (t + 1), :],
            NT,
            preferred_element_type=F32,
            precision=lax.Precision.HIGHEST,
        )
        o_ref[pl.ds(t, 1), :] = got[:1]


def nuggets_of(key, count, nugget, cols):
    ords = nugget.shape[2]
    assert ords <= LANE
    return pl.pallas_call(
        functools.partial(nugget_kernel, (ords, cols)),
        grid_spec=pltpu.PrefetchScalarGridSpec(
            num_scalar_prefetch=2,
            grid=(1,),
            in_specs=[whole(nugget)],
            out_specs=pl.BlockSpec((cols // LANE, LANE), lambda i, *_: (0, 0)),
            scratch_shapes=[pltpu.VMEM((cols, LANE), F32)],
        ),
        out_shape=jax.ShapeDtypeStruct((cols // LANE, LANE), F32),
        compiler_params=pltpu.CompilerParams(vmem_limit_bytes=VMEM),
        name="nuggets",
    )(key, count, nugget)


def factor_kernel(times, pick_ref, tri_ref, w_ref, ld_ref, held):
    tiles = pick_ref.shape[1]
    root = 1.0 / math.sqrt(times)
    u = [pick_ref[x].astype(BF16).astype(F32) * root for x in range(times)]
    nug = pick_ref[times]
    inv = 1.0 / nug
    un = [a * inv for a in u]
    pairs = [(a, b) for a in range(times) for b in range(a, times)]
    prod = jnp.concatenate([un[a] * u[b] for a, b in pairs], axis=0)
    sums = jnp.zeros((prod.shape[0], 2 * LANE), F32)
    for _ in range(3):
        part = prod.astype(BF16)
        sums = sums + jnp.dot(part, tri_ref[...], preferred_element_type=F32)
        prod = prod - part.astype(F32)
    row = lax.broadcasted_iota(jnp.int32, (tiles, LANE), 0)

    def shifted(v, by):
        return jnp.where(row >= by, pltpu.roll(v, by, axis=0), 0.0)

    g = {}
    for i, (a, b) in enumerate(pairs):
        at = slice(tiles * i, tiles * (i + 1))
        before = shifted(sums[at, LANE:], 1)
        by = 1
        while by < tiles:
            before = before + shifted(before, by)
            by *= 2
        g[a, b] = sums[at, :LANE] + before + (1.0 if a == b else 0.0)
    z = list(u)
    quad = jnp.zeros_like(nug)
    scaled = []
    for p in range(times):
        d = 1.0 / g[p, p]
        f = {a: g[p, a] * d for a in range(p + 1, times)}
        for a in range(p + 1, times):
            for b in range(a, times):
                g[a, b] = g[a, b] - f[a] * g[p, b]
            z[a] = z[a] - f[a] * z[p]
        quad = quad + z[p] * z[p] * d
        scaled.append((d, f))
    y = [None] * times
    for p in reversed(range(times)):
        d, f = scaled[p]
        y[p] = z[p] * d
        for b in range(p + 1, times):
            y[p] = y[p] - f[b] * y[b]
    diag = jnp.sqrt(nug + quad)
    over = root / diag
    for x in range(times):
        held[x] = y[x] * over
    for t in range(tiles):
        at = slice(LANE * t, LANE * (t + 1))
        w_ref[:, at] = jnp.concatenate([held[:, t, :]] * ROWS, axis=0).astype(BF16)
        ld_ref[:, at] = jnp.broadcast_to(diag[t : t + 1], (2, LANE))


def factor(picks):
    times, tiles = picks.shape[0] - 1, picks.shape[1]
    assert times % 8 == 0 and tiles == 8
    strict = np.triu(np.ones((LANE, LANE), np.float32), 1)
    tri = jnp.asarray(np.concatenate([strict, np.ones((LANE, LANE), np.float32)], axis=1), BF16)
    return pl.pallas_call(
        functools.partial(factor_kernel, times),
        out_shape=[
            jax.ShapeDtypeStruct((ROWS * times, tiles * LANE), BF16),
            jax.ShapeDtypeStruct((2, tiles * LANE), F32),
        ],
        scratch_shapes=[pltpu.VMEM((times, tiles, LANE), F32)],
        compiler_params=pltpu.CompilerParams(vmem_limit_bytes=VMEM),
        name="factor",
    )(picks, tri)


def panel_kernel(dims, n_parts, key_ref, start_ref, *refs):
    times, ords, deg_local, block, merge = dims
    parts, (mask_ref, w_ref, ld_ref, out_ref, total, lhs, slots, sems) = refs[:n_parts], refs[n_parts:]
    steps = deg_local // block
    cols = ld_ref.shape[1]
    wide = ROWS * times
    windows, tail = divmod(2 * ords, ROWS)
    group = merge * windows * ROWS + (ROWS if tail else 0)

    total[...] = sum(p[0].astype(F32) for p in parts).astype(BF16).astype(F32)

    def out_copy(step):
        slot = lax.rem(step, 2)
        return pltpu.make_async_copy(slots.at[slot], out_ref.at[pl.ds(step * block, block)], sems.at[slot])

    def one_block(step, _):
        o_ref = slots.at[lax.rem(step, 2)]
        for v in range(block // merge):
            at = v * group
            rest = None
            for u in range(merge):
                row = total[pl.ds(step * block + v * merge + u, 1), :]
                for w in range(windows):
                    piece = jnp.broadcast_to(row[:, wide * w : wide * (w + 1)], (ROWS, wide)).astype(BF16)
                    lhs[at : at + ROWS, :] = piece * mask_ref[0]
                    at += ROWS
                if tail:
                    piece = jnp.broadcast_to(row[:, wide * windows : wide * (windows + 1)], (ROWS, wide))
                    piece = piece.astype(BF16) * mask_ref[1 + u]
                    rest = piece if rest is None else rest + piece
            if tail:
                lhs[at : at + ROWS, :] = rest

        @pl.when(step >= 2)
        def _():
            out_copy(step - 2).wait()

        for v in range(block // merge):
            y = jnp.dot(
                lhs[v * group : (v + 1) * group, :], w_ref[...], preferred_element_type=F32
            ).astype(BF16)
            size = windows * ROWS
            for u in range(merge):
                o_ref[v * merge + u, : size // 2] = y[u * size : (u + 1) * size].reshape(size // 2, 2, cols)
            if tail:
                last = y[merge * size :].reshape(ROWS // 2, 2, cols)
                for u in range(merge):
                    o_ref[v * merge + u, size // 2 :] = last[u * tail // 2 : (u + 1) * tail // 2]

        col = lax.broadcasted_iota(jnp.int32, (2, cols), 1)
        part = lax.broadcasted_iota(jnp.int32, (2, cols), 0)

        def chosen_row(e, _):
            k, c, m, l = split_key(key_ref[e], cols, ords)
            l = l - step * block
            old = o_ref[l, m].astype(F32)
            new = jnp.where(col < k, old, jnp.where(col == k, ld_ref[...], 0.0))
            o_ref[l, m] = jnp.where(part == c, new, old).astype(BF16)
            return 0

        lax.fori_loop(start_ref[step], start_ref[step + 1], chosen_row, 0)
        out_copy(step).start()
        return 0

    lax.fori_loop(0, steps, one_block, 0)
    for step in range(max(steps - 2, 0), steps):
        out_copy(step).wait()


def panels(key, starts, parts, weights, diag, dims):
    times, ords, deg_local, block = dims
    cols = diag.shape[1]
    wide = ROWS * times
    windows, tail = divmod(2 * ords, ROWS)
    merge = divisor(block, ROWS // tail if tail else 1)
    row = np.arange(ROWS)[:, None]
    of = np.arange(wide)[None, :] // times
    mask = [row == of] + [(row == tail * u + of) & (of < tail) for u in range(merge if tail else 0)]
    mask = jnp.asarray(np.stack(mask), BF16)
    part_spec = pl.BlockSpec((1,) + parts[0].shape[1:], lambda i, *_: (0, 0, 0))
    rows = block // merge * (merge * windows + (1 if tail else 0)) * ROWS
    return pl.pallas_call(
        functools.partial(panel_kernel, (times, ords, deg_local, block, merge), len(parts)),
        grid_spec=pltpu.PrefetchScalarGridSpec(
            num_scalar_prefetch=2,
            grid=(1,),
            in_specs=[part_spec] * len(parts) + [whole(a) for a in (mask, weights, diag)],
            out_specs=pl.BlockSpec(memory_space=pl.ANY),
            scratch_shapes=[
                pltpu.VMEM(parts[0].shape[1:], F32),
                pltpu.VMEM((rows, wide), BF16),
                pltpu.VMEM((2, block, ords, 2, cols), BF16),
                pltpu.SemaphoreType.DMA((2,)),
            ],
        ),
        out_shape=jax.ShapeDtypeStruct((deg_local, ords, 2, cols), BF16),
        compiler_params=pltpu.CompilerParams(vmem_limit_bytes=VMEM),
        name="panels",
    )(key, starts, *parts, mask, weights, diag)


def in_order(key):
    rank = jnp.sum((key[None, :] < key[:, None]).astype(jnp.int32), axis=1)
    at = jnp.arange(key.shape[0], dtype=jnp.int32)
    return jnp.sum(jnp.where(rank[None, :] == at[:, None], key[None, :], 0), axis=1)


def partner(axis, bit):
    size = lax.axis_size(axis)
    return [(i, i ^ bit) for i in range(size)]


def bits(axis):
    size = lax.axis_size(axis)
    return [1 << s for s in range(size.bit_length() - 1)]


def on_device(fields, legendre, nugget, chosen):
    ords, degs = legendre.shape[1], legendre.shape[2]
    deg_local = nugget.shape[0]
    tm, lat = lax.axis_size("tm"), lax.axis_size("lat")
    cols = chosen.shape[0]
    block = divisor(deg_local, 20)
    me = lax.axis_index("lat")
    ord_start = lax.axis_index("tm") * ords
    deg_start = me * deg_local

    sent = spectra(fields.reshape(-1, fields.shape[-1]), ords, tm)

    k = jnp.arange(cols, dtype=jnp.int32)
    deg = chosen // (2 * tm * ords)
    order = chosen // 2 % (tm * ords) - ord_start
    part = chosen % 2
    mine = (order >= 0) & (order < ords)
    here = mine & (deg >= deg_start) & (deg < deg_start + deg_local)
    none = jnp.int32(2**31 - 1)
    key = jnp.where(mine, make_key(k, part, deg, order, cols, degs), none)
    keyn = jnp.where(here, make_key(k, part, order, deg - deg_start, cols, ords), none)
    steps = div_up(ords, GROUP)
    edge = np.arange(steps + 1) * GROUP << shifts(cols, degs)[2]
    edge = jnp.asarray(np.minimum(edge, 2**31 - 1), jnp.int32)
    groups = jnp.sum((key[None, :] < edge[:, None]).astype(jnp.int32), axis=1)
    edge = jnp.asarray(np.arange(deg_local // block + 1) * block << shifts(cols, ords)[2], jnp.int32)
    starts = jnp.sum((keyn[None, :] < edge[:, None]).astype(jnp.int32), axis=1)
    meta = jnp.concatenate([jnp.stack([me, ord_start]).astype(jnp.int32), groups])
    key, keyn = in_order(key), in_order(keyn)

    nuggets = nuggets_of(keyn, starts[-1:], jnp.transpose(nugget, (0, 2, 1)), cols)
    moved = lax.all_to_all(sent, "tm", split_axis=0, concat_axis=0, tiled=True)
    keep, send, picks = partials(moved, jnp.transpose(legendre, (1, 0, 2)), nuggets, key, meta, lat, cols)
    times = moved.shape[0]
    picks = picks + lax.ppermute(picks, "lat", partner("lat", 1))
    send, picks = lax.optimization_barrier((send, picks))
    parts = [keep, lax.ppermute(send, "lat", partner("lat", 1))]
    for bit in bits("lat")[1:]:
        picks = picks + lax.ppermute(picks, "lat", partner("lat", bit))
        out = sum(p[1::2].astype(F32) for p in parts).astype(BF16)
        parts = [p[0::2] if p.shape[0] > 2 else p for p in parts]
        out, picks = lax.optimization_barrier((out, picks))
        parts.append(lax.ppermute(out, "lat", partner("lat", bit)))
    for bit in bits("tm"):
        picks = picks + lax.ppermute(picks, "tm", partner("tm", bit))
    weights, diag = factor(picks)
    return panels(keyn, starts, parts, weights, diag, (times, ords, deg_local, block))


def solution(mesh):
    placed = (P("tm", "lat", None), P("lat", "tm", None), P("lat", "tm", None), P())
    return jax.shard_map(
        on_device, mesh=mesh, in_specs=placed, out_specs=P("lat", "tm", None, None), check_vma=False
    )
```

time: 129 us -> 96.3 us (0.75)
  between operations: 13.6 us -> 0.14 us
  waiting for transfers between devices: 35.4 us -> 23.3 us
  Pallas kernels: 58.5 us -> 51.1 us
  local copies, waits for them, and re-layouts: 9.7 us -> 5.02 us
  starting transfers between devices: 9.78 us -> 12.7 us
  other arithmetic: 1.96 us -> 3.5 us
    ppermute x5, waiting for transfers between devices: 26.3 us -> 14.7 us  [the longest x3 11.1 us: on_device(): picks = picks + lax.ppermute(picks, 'tm', partner('tm', bit))]
    sort x2 -> x0, local copies, waits for them, and re-layouts: 6.16 us -> none  [on_device(): both = jnp.sort(jnp.stack([key, keyn]), axis=1)]
    pallas_call x1, Pallas kernels: 21.3 us -> 15.1 us  [partials(): pl.pallas_call(functools.partial(partial_kernel, dims), grid_spec=pltpu.P...]
    ppermute x5, starting transfers between devices: 0.39 us -> 3.65 us  [the longest x3 2.06 us: on_device(): picks = picks + lax.ppermute(picks, 'tm', partner('tm', bit))]
    ppermute x1, waiting for transfers between devices: 2.73 us -> 0.01 us  [on_device(): parts = [keep, lax.ppermute(send, 'lat', partner('lat', 1))]]
    unnamed x17 -> x12, local copies, waits for them, and re-layouts: 1.11 us -> 3.43 us
    reduce_sum x0 -> x3, other arithmetic: none -> 2.14 us  [the longest x2 1.11 us: in_order(): rank = jnp.sum((key[None, :] < key[:, None]).astype(jnp.int32), axis=1)]
    all_to_all x1, waiting for transfers between devices: 6.41 us -> 8.52 us  [on_device(): moved = lax.all_to_all(sent, 'tm', split_axis=0, concat_axis=0, tiled=True)]
  transfers between devices with their start and end apart: 8 -> 8, of which waited for: 7 -> 6; matrix products, arithmetic and copies ran while one was open for 3% -> 4% of each run, Pallas kernels for 0% -> 3%
where the time goes in v2:
time: 96.3 us; the launch traced here: 95.7 us
  Pallas kernels  51.1 us (53%)
  waiting for transfers between devices  23.3 us (24%)
  starting transfers between devices  12.7 us (13%)
  local copies, waits for them, and re-layouts  5.02 us (5%)
  other arithmetic  3.5 us (4%)
    pallas_call x1, Pallas kernels, panels(): pl.pallas_call(functools.partial(panel_kernel, (times, ords, deg_local, b...  27.5 us
    pallas_call x1, Pallas kernels, partials(): pl.pallas_call(functools.partial(partial_kernel, dims), grid_spec=pltpu.P...  15.1 us
    ppermute x3, waiting for transfers between devices, on_device(): picks = picks + lax.ppermute(picks, 'tm', partner('tm', bit))  11.1 us
    all_to_all x1, waiting for transfers between devices, on_device(): moved = lax.all_to_all(sent, 'tm', split_axis=0, concat_axis=0, tiled=True)  8.52 us
    all_to_all x1, starting transfers between devices, on_device(): moved = lax.all_to_all(sent, 'tm', split_axis=0, concat_axis=0, tiled=True)  7.25 us
    pallas_call x1, Pallas kernels, spectra(): pl.pallas_call(functools.partial(spectra_kernel, n_lon, ords, rows), grid...  5.55 us
    unnamed x12, local copies, waits for them, and re-layouts  3.43 us
    pallas_call x1, Pallas kernels, nuggets_of(): pl.pallas_call(functools.partial(nugget_kernel, (ords, cols)), grid_spec=...  2.47 us
  transfers between devices with their start and end apart: 8, of which 6 were waited for; matrix products, arithmetic and copies ran while one was open for 4% of the time, Pallas kernels for 3%

profile of v2, /device:TPU:0, one launch (start us, length us, event | category | flops | bytes accessed | tf_op | source)
XLA Modules:
  0.0 95.7 jit_solution(4212628480527104616)
XLA Ops:
  0.0 1.1 %copy-done = bf16[1,180,1440]{2,1,0:T(8,128)(2,1)S(1)} copy-done((bf16[1,180,1440]{2,1,0:T(8,128)(2,1)S(1)}, bf16[1,180,1440]{2,1,0:T(8,128)(2,1)}, u32[]{:S(2)}) %copy-start) | copy-done | bytes 518424
  1.1 5.5 %spectra.1 = bf16[8,96,384]{2,1,0:T(8,128)(2,1)} custom-call(bf16[180,1440]{1,0:T(8,128)(2,1)S(1)} %bitcast.5), custom_call_target="tpu_custom_call" | custom-call | tf_op jit(solution)/shard_map/spectra/pallas_call | solution.py:100
  6.6 7.3 %all-to-all-start = ((bf16[8,96,384]{2,1,0:T(8,128)(2,1)}), bf16[8,96,384]{2,1,0:T(8,128)(2,1)S(1)}, u32[]{:S(2)}, u32[]{:S(2)}) async-start(bf16[8,96,384]{2,1,0:T(8,128)(2,1)} %spectra.1), calls=%async_computation | async-start | bytes 1179648 | tf_op jit(solution)/shard_map/all_to_all | solution.py:489
  13.9 0.7 or_select_fusion
  14.6 0.2 convert_reduce_fusion.2.start_ref
  14.8 0.6 slice.11.count_ref
  15.4 0.6 convert_reduce_fusion.1
  16.0 0.6 convert_reduce_fusion
  16.5 1.0 %select_reduce_fusion = (s32[1024]{0:T(1024)S(1)}, s32[1024]{0:T(1024)S(1)}) fusion(s32[1024]{0:T(1024)S(1)} %convert_reduce_fusion, s32[1024]{0:T(1024)S(1)} %get-tuple-element.23, s32[1024]{0:T(1024)S(1)} %get-tuple-element.24, s32[1024]{0:T(1024)S(1)} %convert_reduce_fusion.1), kind=kLoop, calls=%fused_computation | loop fusion | flops 6289408 | bytes 24576 | tf_op jit(solution)/shard_map/reduce_sum | solution.py:445
  17.6 0.9 copy-done.1
  18.5 2.5 %nuggets.1.nug_ref = f32[8,128]{1,0:T(8,128)S(1)} custom-call(s32[1024]{0:T(1024)S(1)} %get-tuple-element.26.key_ref, s32[1]{0:T(128)} %slice.11.count_ref, f32[180,2,90]{2,1,0:T(2,128)S(1)} %bitcast.6), custom_call_target="tpu_custom_call" | custom-call | tf_op jit(solution)/shard_map/nuggets/pallas_call | solution.py:253
  20.9 0.2 convert_reduce_fusion.3
  21.2 0.1 pad_add_fusion.meta_ref
  21.2 8.5 %all-to-all-done.x_ref = bf16[8,96,384]{2,1,0:T(8,128)(2,1)S(1)} async-done(((bf16[8,96,384]{2,1,0:T(8,128)(2,1)}), bf16[8,96,384]{2,1,0:T(8,128)(2,1)S(1)}, u32[]{:S(2)}, u32[]{:S(2)}) %all-to-all-start) | async-done | bytes 589856 | tf_op jit(solution)/shard_map/all_to_all | solution.py:489
  29.8 0.8 copy-done.3
  30.5 0.7 copy-done.5
  31.2 15.1 %partials.1 = (bf16[2,180,1536]{2,1,0:T(8,128)(2,1)S(1)}, bf16[2,180,1536]{2,1,0:T(8,128)(2,1)S(1)}, f32[9,8,128]{2,1,0:T(8,128)S(1)}) custom-call(s32[1024]{0:T(1024)S(1)} %get-tuple-element.25.key_ref, s32[9]{0:T(128)S(1)} %pad_add_fusion.meta_ref, bf16[8,96,384]{2,1,0:T(8,128)(2,1)S(1)} %all-to-all-done.x_ref, bf16[90,180,720]{2,1,0:T(8,128)(2,1)} %bitcast.7, ...), custom_call_target="tpu_custom_call" | custom-call | tf_op jit(solution)/shard_map/partials/pallas_call | solution.py:198
  46.5 1.2 %collective-permute-done = f32[9,8,128]{2,1,0:T(8,128)S(1)} collective-permute-done((f32[9,8,128]{2,1,0:T(8,128)S(1)}, f32[9,8,128]{2,1,0:T(8,128)S(1)}, u32[]{:S(2)}, u32[]{:S(2)}) %collective-permute-start) | collective-permute-done | bytes 36896 | tf_op jit(solution)/shard_map/ppermute | solution.py:492
  47.7 0.9 copy.14
  48.5 0.2 collective-permute-start.1
  48.7 1.5 %collective-permute-start.2 = (f32[9,8,128]{2,1,0:T(8,128)S(1)}, f32[9,8,128]{2,1,0:T(8,128)S(1)}, u32[]{:S(2)}, u32[]{:S(2)}) collective-permute-start(f32[9,8,128]{2,1,0:T(8,128)S(1)} %add.36), channel_id=1, source_target_pairs={{0,2},{1,3},{2,0},{3,1},{4,6},{5,7},{6,4},{7,5},{8,10},{9,11},{10,... | collective-permute-start | bytes 110600 | tf_op jit(solution)/shard_map/ppermute | solution.py:496
  50.3 2.4 %collective-permute-done.2 = f32[9,8,128]{2,1,0:T(8,128)S(1)} collective-permute-done((f32[9,8,128]{2,1,0:T(8,128)S(1)}, f32[9,8,128]{2,1,0:T(8,128)S(1)}, u32[]{:S(2)}, u32[]{:S(2)}) %collective-permute-start.2) | collective-permute-done | bytes 36896 | tf_op jit(solution)/shard_map/ppermute | solution.py:496
  52.7 0.1 copy.16.refs_1_
  52.8 0.1 add_convert_fusion
  53.0 1.6 %collective-permute-start.3 = (bf16[1,180,1536]{2,1,0:T(8,128)(2,1)S(1)}, bf16[1,180,1536]{2,1,0:T(8,128)(2,1)S(1)}, u32[]{:S(2)}, u32[]{:S(2)}) collective-permute-start(bf16[1,180,1536]{2,1,0:T(8,128)(2,1)S(1)} %add_convert_fusion), channel_id=1, source_target_pairs={{0,2},{1,3},{2,0},{3,1},{4,6},{5,7},{6,4},{7,5},{8,10},{9,11},{10,... | collective-permute-start | bytes 1658888 | tf_op jit(solution)/shard_map/ppermute | solution.py:500
  54.6 1.6 %collective-permute-start.4 = (f32[9,8,128]{2,1,0:T(8,128)S(1)}, f32[9,8,128]{2,1,0:T(8,128)S(1)}, u32[]{:S(2)}, u32[]{:S(2)}) collective-permute-start(f32[9,8,128]{2,1,0:T(8,128)S(1)} %add.38), channel_id=1, source_target_pairs={{0,4},{4,0},{8,12},{12,8},{16,20},{20,16},{24,28},{28,24},{1,5},{5... | collective-permute-start | bytes 110600 | tf_op jit(solution)/shard_map/ppermute | solution.py:502
  56.2 2.3 %collective-permute-done.4 = f32[9,8,128]{2,1,0:T(8,128)S(1)} collective-permute-done((f32[9,8,128]{2,1,0:T(8,128)S(1)}, f32[9,8,128]{2,1,0:T(8,128)S(1)}, u32[]{:S(2)}, u32[]{:S(2)}) %collective-permute-start.4) | collective-permute-done | bytes 36896 | tf_op jit(solution)/shard_map/ppermute | solution.py:502
  58.5 0.4 collective-permute-start.5
  59.0 3.5 %collective-permute-done.5 = f32[9,8,128]{2,1,0:T(8,128)S(1)} collective-permute-done((f32[9,8,128]{2,1,0:T(8,128)S(1)}, f32[9,8,128]{2,1,0:T(8,128)S(1)}, u32[]{:S(2)}, u32[]{:S(2)}) %collective-permute-start.5) | collective-permute-done | bytes 36896 | tf_op jit(solution)/shard_map/ppermute | solution.py:502
  62.5 5.2 %collective-permute-done.6 = f32[9,8,128]{2,1,0:T(8,128)S(1)} collective-permute-done((f32[9,8,128]{2,1,0:T(8,128)S(1)}, f32[9,8,128]{2,1,0:T(8,128)S(1)}, u32[]{:S(2)}, u32[]{:S(2)}) %collective-permute-start.6) | collective-permute-done | bytes 36896 | tf_op jit(solution)/shard_map/ppermute | solution.py:502
  67.8 0.4 factor.1
  68.2 27.5 %panels.1 = bf16[180,90,2,1024]{3,2,1,0:T(2,128)(2,1)} custom-call(s32[1024]{0:T(1024)S(1)} %get-tuple-element.26.key_ref, s32[10]{0:T(128)S(1)} %convert_reduce_fusion.2.start_ref, bf16[2,180,1536]{2,1,0:T(8,128)(2,1)S(1)} %get-tuple-element.14.refs_0_, bf16[2,180,1536]{2,1,0:T(8,128)(2,1)S(1)} %copy.16.refs_1_, ...), custom_call_target="tpu_custom_call" | custom-call | tf_op jit(solution)/shard_map/panels/pallas_call | solution.py:422
  (19 shorter events, 0.1 us)
Async XLA Ops:
  0.0 1.1 %copy-start = (bf16[1,180,1440]{2,1,0:T(8,128)(2,1)S(1)}, bf16[1,180,1440]{2,1,0:T(8,128)(2,1)}, u32[]{:S(2)}) copy-start(bf16[1,180,1440]{2,1,0:T(8,128)(2,1)} %param.10) | copy-start | bytes 1555204
  6.6 23.1 %all-to-all-start = ((bf16[8,96,384]{2,1,0:T(8,128)(2,1)}), bf16[8,96,384]{2,1,0:T(8,128)(2,1)S(1)}, u32[]{:S(2)}, u32[]{:S(2)}) async-start(bf16[8,96,384]{2,1,0:T(8,128)(2,1)} %spectra.1), calls=%async_computation | async-start | bytes 1179648 | tf_op jit(solution)/shard_map/all_to_all | solution.py:489
  17.6 0.9 copy-start.1
  29.8 0.8 copy-start.3
  30.5 0.7 copy-start.5
  46.3 21.4 %copy-start.2 = (bf16[128,256]{1,0:T(8,128)(2,1)S(1)}, bf16[128,256]{1,0:T(8,128)(2,1)}, u32[]{:S(2)}) copy-start(bf16[128,256]{1,0:T(8,128)(2,1)} %constant.84.clone.tri_ref) | copy-start | bytes 196612
  46.4 21.8 %copy-start.4 = (bf16[5,16,128]{2,1,0:T(8,128)(2,1)S(1)}, bf16[5,16,128]{2,1,0:T(8,128)(2,1)}, u32[]{:S(2)}) copy-start(bf16[5,16,128]{2,1,0:T(8,128)(2,1)} %constant.85.clone.refs_3_) | copy-start | bytes 61444
  46.4 1.3 %collective-permute-start = (f32[9,8,128]{2,1,0:T(8,128)S(1)}, f32[9,8,128]{2,1,0:T(8,128)S(1)}, u32[]{:S(2)}, u32[]{:S(2)}) collective-permute-start(f32[9,8,128]{2,1,0:T(8,128)S(1)} %get-tuple-element.16), channel_id=1, source_target_pairs={{0,1},{1,0},{2,3},{3,2},{4,5},{5,4},{6,7},{7,6},{8,9},{9,8},{10,11... | collective-permute-start | bytes 110600 | tf_op jit(solution)/shard_map/ppermute | solution.py:492
  48.5 4.2 %collective-permute-start.1 = (bf16[2,180,1536]{2,0,1:T(2,128)(2,1)S(1)}, bf16[2,180,1536]{2,0,1:T(2,128)(2,1)S(1)}, u32[]{:S(2)}, u32[]{:S(2)}) collective-permute-start(bf16[2,180,1536]{2,0,1:T(2,128)(2,1)S(1)} %copy.14), channel_id=1, source_target_pairs={{0,1},{1,0},{2,3},{3,2},{4,5},{5,4},{6,7},{7,6},{8,9},{9,8},{10,11... | collective-permute-start | bytes 3317768 | tf_op jit(solution)/shard_map/ppermute | solution.py:494
  48.7 4.0 %collective-permute-start.2 = (f32[9,8,128]{2,1,0:T(8,128)S(1)}, f32[9,8,128]{2,1,0:T(8,128)S(1)}, u32[]{:S(2)}, u32[]{:S(2)}) collective-permute-start(f32[9,8,128]{2,1,0:T(8,128)S(1)} %add.36), channel_id=1, source_target_pairs={{0,2},{1,3},{2,0},{3,1},{4,6},{5,7},{6,4},{7,5},{8,10},{9,11},{10,... | collective-permute-start | bytes 110600 | tf_op jit(solution)/shard_map/ppermute | solution.py:496
  53.0 15.2 %collective-permute-start.3 = (bf16[1,180,1536]{2,1,0:T(8,128)(2,1)S(1)}, bf16[1,180,1536]{2,1,0:T(8,128)(2,1)S(1)}, u32[]{:S(2)}, u32[]{:S(2)}) collective-permute-start(bf16[1,180,1536]{2,1,0:T(8,128)(2,1)S(1)} %add_convert_fusion), channel_id=1, source_target_pairs={{0,2},{1,3},{2,0},{3,1},{4,6},{5,7},{6,4},{7,5},{8,10},{9,11},{10,... | collective-permute-start | bytes 1658888 | tf_op jit(solution)/shard_map/ppermute | solution.py:500
  54.6 4.0 %collective-permute-start.4 = (f32[9,8,128]{2,1,0:T(8,128)S(1)}, f32[9,8,128]{2,1,0:T(8,128)S(1)}, u32[]{:S(2)}, u32[]{:S(2)}) collective-permute-start(f32[9,8,128]{2,1,0:T(8,128)S(1)} %add.38), channel_id=1, source_target_pairs={{0,4},{4,0},{8,12},{12,8},{16,20},{20,16},{24,28},{28,24},{1,5},{5... | collective-permute-start | bytes 110600 | tf_op jit(solution)/shard_map/ppermute | solution.py:502
  58.5 4.0 %collective-permute-start.5 = (f32[9,8,128]{2,1,0:T(8,128)S(1)}, f32[9,8,128]{2,1,0:T(8,128)S(1)}, u32[]{:S(2)}, u32[]{:S(2)}) collective-permute-start(f32[9,8,128]{2,1,0:T(8,128)S(1)} %add.39), channel_id=1, source_target_pairs={{0,8},{4,12},{8,0},{12,4},{16,24},{20,28},{24,16},{28,20},{1,9},{5... | collective-permute-start | bytes 110600 | tf_op jit(solution)/shard_map/ppermute | solution.py:502
  62.5 5.3 %collective-permute-start.6 = (f32[9,8,128]{2,1,0:T(8,128)S(1)}, f32[9,8,128]{2,1,0:T(8,128)S(1)}, u32[]{:S(2)}, u32[]{:S(2)}) collective-permute-start(f32[9,8,128]{2,1,0:T(8,128)S(1)} %add.40), channel_id=1, source_target_pairs={{0,16},{4,20},{8,24},{12,28},{16,0},{20,4},{24,8},{28,12},{1,17},{... | collective-permute-start | bytes 110600 | tf_op jit(solution)/shard_map/ppermute | solution.py:502

commit v3 on v2

--- a/solution.py
+++ b/solution.py
@@ -11,8 +11,10 @@
 
 LANE = 128
 ROWS = 16
+DESTS = 8
 GROUP = 16
 VMEM = 48 << 20
+MOST = 58 << 20
 F32, BF16 = jnp.float32, jnp.bfloat16
 NT = (((1,), (1,)), ((), ()))
 
@@ -60,18 +62,27 @@
     return cos, sin
 
 
-def spectra_kernel(n_lon, ords, rows, f_ref, o_ref, c_ref, s_ref):
-    dest = pl.program_id(0)
+def spectra_kernel(n_lon, ords, rows, f_hbm, o_ref, table, f_ref, sem):
+    step = pl.program_id(0)
+    per = o_ref.shape[0]
     lats = f_ref.shape[0]
     tiles = rows // 8
-    lane = lax.broadcasted_iota(jnp.int32, (tiles, 2 * LANE), 1)
-    lane = jnp.where(lane < LANE, lane, LANE).astype(F32)
-    first = (dest * ords + 8 * lax.broadcasted_iota(jnp.int32, (tiles, 2 * LANE), 0)).astype(F32)
+
+    @pl.when(step == 0)
+    def _():
+        pltpu.make_async_copy(f_hbm, f_ref, sem).start()
+
+    shape = (per * tiles, 2 * LANE)
+    lane = lax.broadcasted_iota(jnp.int32, shape, 1)
+    lane = jnp.minimum(lane, LANE).astype(F32)
+    tile = lax.broadcasted_iota(jnp.int32, shape, 0)
+    of = sum((tile >= tiles * d).astype(jnp.int32) for d in range(1, per)) if per > 1 else 0
+    first = ((step * per + of) * ords + 8 * (tile - tiles * of)).astype(F32)
     pc, ps = turn(first * lane, n_lon)
     few = lax.broadcasted_iota(jnp.int32, (8, 2 * LANE), 0).astype(F32)
     qc, qs = turn(few * lane[:1], n_lon)
     scale = 1.0 / math.sqrt(n_lon)
-    for p in range(0, tiles, 2):
+    for p in range(0, per * tiles, 2):
         both_c, both_s = [], []
         for i in (p, p + 1):
             both_c.append(pc[i : i + 1] * qc - ps[i : i + 1] * qs)
@@ -80,37 +91,50 @@
         sin = jnp.concatenate(both_s, axis=0)
         rc, rs = cos[:, LANE:], sin[:, LANE:]
         c, s = cos[:, :LANE] * scale, sin[:, :LANE] * scale
+        d, r = divmod(8 * p, rows)
+        at_c, at_s = 2 * d * rows + r, (2 * d + 1) * rows + r
         for a in range(div_up(n_lon, LANE)):
             width = min(LANE, n_lon - a * LANE)
-            at = (slice(8 * p, 8 * p + 16), slice(a * LANE, a * LANE + width))
-            c_ref[at] = c[:, :width].astype(BF16)
-            s_ref[at] = (-s[:, :width]).astype(BF16)
+            at = slice(a * LANE, a * LANE + width)
+            table[at_c : at_c + 16, at] = c[:, :width].astype(BF16)
+            table[at_s : at_s + 16, at] = (-s[:, :width]).astype(BF16)
             c, s = c * rc - s * rs, s * rc + c * rs
-    f = f_ref[...]
-    re = lax.dot_general(c_ref[...], f, NT, preferred_element_type=F32)
-    im = lax.dot_general(s_ref[...], f, NT, preferred_element_type=F32)
+
+    @pl.when(step == 0)
+    def _():
+        pltpu.make_async_copy(f_hbm, f_ref, sem).wait()
+
     pad = jnp.zeros((rows, o_ref.shape[2] - 2 * lats), F32)
-    o_ref[0] = jnp.concatenate([re, im, pad], axis=1).astype(BF16)
+    y = lax.dot_general(table[...], f_ref[...], NT, preferred_element_type=F32)
+    for d in range(per):
+        re = y[2 * d * rows : (2 * d + 1) * rows]
+        im = y[(2 * d + 1) * rows : (2 * d + 2) * rows]
+        o_ref[d] = jnp.concatenate([re, im, pad], axis=1).astype(BF16)
 
 
 def spectra(fields, ords, dests):
     lats, n_lon = fields.shape
     rows = div_up(ords, GROUP) * GROUP
     lanes = div_up(2 * lats, LANE) * LANE
+    per = divisor(dests, DESTS)
     return pl.pallas_call(
         functools.partial(spectra_kernel, n_lon, ords, rows),
-        grid=(dests,),
-        in_specs=[pl.BlockSpec((lats, n_lon), lambda i: (0, 0))],
-        out_specs=pl.BlockSpec((1, rows, lanes), lambda i: (i, 0, 0)),
+        grid=(dests // per,),
+        in_specs=[pl.BlockSpec(memory_space=pl.ANY)],
+        out_specs=pl.BlockSpec((per, rows, lanes), lambda i: (i, 0, 0)),
         out_shape=jax.ShapeDtypeStruct((dests, rows, lanes), BF16),
-        scratch_shapes=[pltpu.VMEM((rows, n_lon), BF16), pltpu.VMEM((rows, n_lon), BF16)],
-        compiler_params=pltpu.CompilerParams(vmem_limit_bytes=VMEM),
+        scratch_shapes=[
+            pltpu.VMEM((2 * per * rows, n_lon), BF16),
+            pltpu.VMEM((lats, n_lon), BF16),
+            pltpu.SemaphoreType.DMA,
+        ],
+        compiler_params=pltpu.CompilerParams(vmem_limit_bytes=MOST),
         name="spectra",
     )(fields)
 
 
 def partial_kernel(
-    dims, key_ref, meta_ref, x_ref, leg_ref, nug_ref, perm_ref, sel_ref,
+    dims, key_ref, meta_ref, x_ref, leg_ref, nug_ref,
     keep_ref, send_ref, pick_ref, flat, turned, held,
 ):
     times, lats, ords, degs, blocks, deg_local, cols = dims
@@ -125,7 +149,11 @@
         held[...] = jnp.zeros_like(held)
 
     x = x_ref[...].reshape(times * GROUP, x_ref.shape[2])
-    x = jnp.dot(perm_ref[...], x, preferred_element_type=F32)
+    n = times * GROUP
+    to = lax.broadcasted_iota(jnp.int32, (n, n), 0)
+    of = lax.broadcasted_iota(jnp.int32, (n, n), 1)
+    perm = (of == lax.rem(to, times) * GROUP + to // times).astype(F32).astype(BF16)
+    x = jnp.dot(perm, x, preferred_element_type=F32)
     re = x[:, :lats]
     im = x[:, lats : 2 * lats]
     deg = lax.broadcasted_iota(jnp.int32, (width, degs), 1)
@@ -152,11 +180,11 @@
 
         @pl.when(where % 2 == 0)
         def _():
-            keep_ref[where // 2] = part
+            keep_ref[where // 2, :deg_local] = part
 
         @pl.when(where % 2 == 1)
         def _():
-            send_ref[where // 2] = part
+            send_ref[where // 2, :deg_local] = part
 
     lane = lax.broadcasted_iota(jnp.int32, (1, lanes), 1)
 
@@ -171,10 +199,12 @@
 
     @pl.when(step == steps - 1)
     def _():
+        sel = lax.rem(lax.broadcasted_iota(jnp.int32, (times, lanes), 1), times)
+        sel = (sel == lax.broadcasted_iota(jnp.int32, (times, lanes), 0)).astype(F32).astype(BF16)
         for t in range(cols // LANE):
             at = slice(LANE * t, LANE * (t + 1))
             pick_ref[:times, t, :] = lax.dot_general(
-                sel_ref[...], held[at, :].astype(BF16), NT, preferred_element_type=F32
+                sel, held[at, :].astype(BF16), NT, preferred_element_type=F32
             )
         pick_ref[times] = nug_ref[...]
 
@@ -185,15 +215,9 @@
     deg_local = degs // blocks
     lanes = GROUP * 2 * times
     steps = rows // GROUP
-    n = times * GROUP
-    perm = np.zeros((GROUP, times, times, GROUP), np.float32)
-    for t in range(times):
-        for m in range(GROUP):
-            perm[m, t, t, m] = 1
-    perm = jnp.asarray(perm.reshape(n, n), BF16)
-    sel = jnp.asarray(np.tile(np.eye(times, dtype=np.float32), (1, 2 * GROUP)), BF16)
-    half = jax.ShapeDtypeStruct((blocks // 2, deg_local, steps * lanes), BF16)
-    half_spec = pl.BlockSpec((blocks // 2, deg_local, lanes), lambda i, *_: (0, 0, i))
+    held_rows = div_up(deg_local, 8) * 8
+    half = jax.ShapeDtypeStruct((blocks // 2, held_rows, steps * lanes), BF16)
+    half_spec = pl.BlockSpec((blocks // 2, held_rows, lanes), lambda i, *_: (0, 0, i))
     dims = (times, lats, ords, degs, blocks, deg_local, cols)
     return pl.pallas_call(
         functools.partial(partial_kernel, dims),
@@ -204,8 +228,6 @@
                 pl.BlockSpec((times, GROUP, width), lambda i, *_: (0, i, 0)),
                 pl.BlockSpec((GROUP, lats, degs), lambda i, *_: (i, 0, 0)),
                 whole(nuggets),
-                whole(perm),
-                whole(sel),
             ],
             out_specs=[
                 half_spec,
@@ -221,7 +243,7 @@
         out_shape=[half, half, jax.ShapeDtypeStruct((times + 1, cols // LANE, LANE), F32)],
         compiler_params=pltpu.CompilerParams(vmem_limit_bytes=VMEM),
         name="partials",
-    )(key, meta, moved, legendre, nuggets, perm, sel)
+    )(key, meta, moved, legendre, nuggets)
 
 
 def nugget_kernel(dims, key_ref, count_ref, nug_ref, o_ref, held):
@@ -338,28 +360,51 @@
     )(picks, tri)
 
 
+def blocks_of(count):
+    if count % 20 == 0 and count >= 60:
+        return 8, 20, 12, count // 20 - 1
+    size = divisor(count, 20)
+    assert count // size >= 3
+    return size, size, size, count // size - 2
+
+
+def block_edges(count):
+    first, middle, last, n = blocks_of(count)
+    return np.cumsum([0, first] + [middle] * n + [last])
+
+
+def merged(size, tail):
+    return divisor(size, ROWS // tail if tail else 1)
+
+
 def panel_kernel(dims, n_parts, key_ref, start_ref, *refs):
-    times, ords, deg_local, block, merge = dims
+    times, ords, deg_local = dims
     parts, (mask_ref, w_ref, ld_ref, out_ref, total, lhs, slots, sems) = refs[:n_parts], refs[n_parts:]
-    steps = deg_local // block
     cols = ld_ref.shape[1]
     wide = ROWS * times
     windows, tail = divmod(2 * ords, ROWS)
-    group = merge * windows * ROWS + (ROWS if tail else 0)
+    first, middle, last, n_middle = blocks_of(deg_local)
 
     total[...] = sum(p[0].astype(F32) for p in parts).astype(BF16).astype(F32)
 
-    def out_copy(step):
-        slot = lax.rem(step, 2)
-        return pltpu.make_async_copy(slots.at[slot], out_ref.at[pl.ds(step * block, block)], sems.at[slot])
-
-    def one_block(step, _):
-        o_ref = slots.at[lax.rem(step, 2)]
-        for v in range(block // merge):
+    def out_copy(b, low, size):
+        slot = b % 2 if isinstance(b, int) else lax.rem(b, 2)
+        return pltpu.make_async_copy(
+            slots.at[slot, pl.ds(0, size)], out_ref.at[pl.ds(low, size)], sems.at[slot]
+        )
+
+    def middle_copy(i):
+        return out_copy(1 + i, first + middle * i, middle)
+
+    def do_block(b, low, size, wait):
+        merge = merged(size, tail)
+        group = merge * windows * ROWS + (ROWS if tail else 0)
+        o_ref = slots.at[b % 2 if isinstance(b, int) else lax.rem(b, 2)]
+        for v in range(size // merge):
             at = v * group
             rest = None
             for u in range(merge):
-                row = total[pl.ds(step * block + v * merge + u, 1), :]
+                row = total[pl.ds(low + v * merge + u, 1), :]
                 for w in range(windows):
                     piece = jnp.broadcast_to(row[:, wide * w : wide * (w + 1)], (ROWS, wide)).astype(BF16)
                     lhs[at : at + ROWS, :] = piece * mask_ref[0]
@@ -371,56 +416,75 @@
             if tail:
                 lhs[at : at + ROWS, :] = rest
 
-        @pl.when(step >= 2)
-        def _():
-            out_copy(step - 2).wait()
-
-        for v in range(block // merge):
+        wait()
+        for v in range(size // merge):
             y = jnp.dot(
                 lhs[v * group : (v + 1) * group, :], w_ref[...], preferred_element_type=F32
             ).astype(BF16)
-            size = windows * ROWS
+            full = windows * ROWS
             for u in range(merge):
-                o_ref[v * merge + u, : size // 2] = y[u * size : (u + 1) * size].reshape(size // 2, 2, cols)
+                o_ref[v * merge + u, : full // 2] = y[u * full : (u + 1) * full].reshape(full // 2, 2, cols)
             if tail:
-                last = y[merge * size :].reshape(ROWS // 2, 2, cols)
+                ends = y[merge * full :].reshape(ROWS // 2, 2, cols)
                 for u in range(merge):
-                    o_ref[v * merge + u, size // 2 :] = last[u * tail // 2 : (u + 1) * tail // 2]
+                    o_ref[v * merge + u, full // 2 :] = ends[u * tail // 2 : (u + 1) * tail // 2]
 
         col = lax.broadcasted_iota(jnp.int32, (2, cols), 1)
         part = lax.broadcasted_iota(jnp.int32, (2, cols), 0)
 
         def chosen_row(e, _):
             k, c, m, l = split_key(key_ref[e], cols, ords)
-            l = l - step * block
+            l = l - low
             old = o_ref[l, m].astype(F32)
             new = jnp.where(col < k, old, jnp.where(col == k, ld_ref[...], 0.0))
             o_ref[l, m] = jnp.where(part == c, new, old).astype(BF16)
             return 0
 
-        lax.fori_loop(start_ref[step], start_ref[step + 1], chosen_row, 0)
-        out_copy(step).start()
+        lax.fori_loop(start_ref[b], start_ref[b + 1], chosen_row, 0)
+        out_copy(b, low, size).start()
+
+    def middle_block(i, _):
+        def wait():
+            @pl.when(i == 1)
+            def _():
+                out_copy(0, 0, first).wait()
+
+            @pl.when(i >= 2)
+            def _():
+                middle_copy(i - 2).wait()
+
+        do_block(1 + i, first + middle * i, middle, wait)
         return 0
 
-    lax.fori_loop(0, steps, one_block, 0)
-    for step in range(max(steps - 2, 0), steps):
-        out_copy(step).wait()
+    do_block(0, 0, first, lambda: None)
+    lax.fori_loop(0, n_middle, middle_block, 0)
+
+    def wait_last():
+        if n_middle >= 2:
+            middle_copy(n_middle - 2).wait()
+        else:
+            out_copy(0, 0, first).wait()
+
+    do_block(1 + n_middle, first + middle * n_middle, last, wait_last)
+    middle_copy(n_middle - 1).wait()
+    out_copy(1 + n_middle, first + middle * n_middle, last).wait()
 
 
 def panels(key, starts, parts, weights, diag, dims):
-    times, ords, deg_local, block = dims
+    times, ords, deg_local = dims
     cols = diag.shape[1]
     wide = ROWS * times
     windows, tail = divmod(2 * ords, ROWS)
-    merge = divisor(block, ROWS // tail if tail else 1)
+    sizes = blocks_of(deg_local)[:3]
+    most = max(merged(size, tail) for size in sizes)
     row = np.arange(ROWS)[:, None]
     of = np.arange(wide)[None, :] // times
-    mask = [row == of] + [(row == tail * u + of) & (of < tail) for u in range(merge if tail else 0)]
+    mask = [row == of] + [(row == tail * u + of) & (of < tail) for u in range(most if tail else 0)]
     mask = jnp.asarray(np.stack(mask), BF16)
     part_spec = pl.BlockSpec((1,) + parts[0].shape[1:], lambda i, *_: (0, 0, 0))
-    rows = block // merge * (merge * windows + (1 if tail else 0)) * ROWS
+    rows = max(size // merged(size, tail) * (merged(size, tail) * windows + (1 if tail else 0)) for size in sizes)
     return pl.pallas_call(
-        functools.partial(panel_kernel, (times, ords, deg_local, block, merge), len(parts)),
+        functools.partial(panel_kernel, dims, len(parts)),
         grid_spec=pltpu.PrefetchScalarGridSpec(
             num_scalar_prefetch=2,
             grid=(1,),
@@ -428,8 +492,8 @@
             out_specs=pl.BlockSpec(memory_space=pl.ANY),
             scratch_shapes=[
                 pltpu.VMEM(parts[0].shape[1:], F32),
-                pltpu.VMEM((rows, wide), BF16),
-                pltpu.VMEM((2, block, ords, 2, cols), BF16),
+                pltpu.VMEM((rows * ROWS, wide), BF16),
+                pltpu.VMEM((2, max(sizes), ords, 2, cols), BF16),
                 pltpu.SemaphoreType.DMA((2,)),
             ],
         ),
@@ -460,7 +524,6 @@
     deg_local = nugget.shape[0]
     tm, lat = lax.axis_size("tm"), lax.axis_size("lat")
     cols = chosen.shape[0]
-    block = divisor(deg_local, 20)
     me = lax.axis_index("lat")
     ord_start = lax.axis_index("tm") * ords
     deg_start = me * deg_local
@@ -480,7 +543,7 @@
     edge = np.arange(steps + 1) * GROUP << shifts(cols, degs)[2]
     edge = jnp.asarray(np.minimum(edge, 2**31 - 1), jnp.int32)
     groups = jnp.sum((key[None, :] < edge[:, None]).astype(jnp.int32), axis=1)
-    edge = jnp.asarray(np.arange(deg_local // block + 1) * block << shifts(cols, ords)[2], jnp.int32)
+    edge = jnp.asarray(block_edges(deg_local) << shifts(cols, ords)[2], jnp.int32)
     starts = jnp.sum((keyn[None, :] < edge[:, None]).astype(jnp.int32), axis=1)
     meta = jnp.concatenate([jnp.stack([me, ord_start]).astype(jnp.int32), groups])
     key, keyn = in_order(key), in_order(keyn)
@@ -501,7 +564,7 @@
     for bit in bits("tm"):
         picks = picks + lax.ppermute(picks, "tm", partner("tm", bit))
     weights, diag = factor(picks)
-    return panels(keyn, starts, parts, weights, diag, (times, ords, deg_local, block))
+    return panels(keyn, starts, parts, weights, diag, (times, ords, deg_local))
 
 
 def solution(mesh):

time: 96.3 us -> 91.3 us (0.948)
  local copies, waits for them, and re-layouts: 5.02 us -> 1.54 us
  Pallas kernels: 51.1 us -> 50 us
    unnamed x12 -> x6, local copies, waits for them, and re-layouts: 3.43 us -> 0.93 us
    pallas_call x1, Pallas kernels: 5.55 us -> 4.11 us  [spectra(): pl.pallas_call(functools.partial(spectra_kernel, n_lon, ords, rows), grid...]
  transfers between devices with their start and end apart: 8 -> 8, of which waited for: 6 -> 6; matrix products, arithmetic and copies ran while one was open for 4% -> 5% of each run, Pallas kernels for 3% -> 3%
where the time goes in v3:
time: 91.3 us; the launch traced here: 91 us
  Pallas kernels  50 us (55%)
  waiting for transfers between devices  23.1 us (25%)
  starting transfers between devices  11.9 us (13%)
  other arithmetic  4.15 us (5%)
  local copies, waits for them, and re-layouts  1.54 us (2%)
    pallas_call x1, Pallas kernels, panels(): pl.pallas_call(functools.partial(panel_kernel, dims, len(parts)), grid_sp...  27.5 us
    pallas_call x1, Pallas kernels, partials(): pl.pallas_call(functools.partial(partial_kernel, dims), grid_spec=pltpu.P...  15.4 us
    ppermute x3, waiting for transfers between devices, on_device(): picks = picks + lax.ppermute(picks, 'tm', partner('tm', bit))  11.8 us
    all_to_all x1, waiting for transfers between devices, on_device(): moved = lax.all_to_all(sent, 'tm', split_axis=0, concat_axis=0, tiled=True)  7.7 us
    all_to_all x1, starting transfers between devices, on_device(): moved = lax.all_to_all(sent, 'tm', split_axis=0, concat_axis=0, tiled=True)  7.27 us
    pallas_call x1, Pallas kernels, spectra(): pl.pallas_call(functools.partial(spectra_kernel, n_lon, ords, rows), grid...  4.11 us
    pallas_call x1, Pallas kernels, nuggets_of(): pl.pallas_call(functools.partial(nugget_kernel, (ords, cols)), grid_spec=...  2.65 us
    ppermute x1, waiting for transfers between devices, on_device(): picks = picks + lax.ppermute(picks, 'lat', partner('lat', bit))  2.43 us
  transfers between devices with their start and end apart: 8, of which 6 were waited for; matrix products, arithmetic and copies ran while one was open for 5% of the time, Pallas kernels for 3%

profile of v3, /device:TPU:0, one launch (start us, length us, event | category | flops | bytes accessed | tf_op | source)
XLA Modules:
  0.0 91.0 jit_solution(6538930995269235057)
XLA Ops:
  0.0 4.1 %spectra.1 = bf16[8,96,384]{2,1,0:T(8,128)(2,1)} custom-call(bf16[180,1440]{1,0:T(8,128)(2,1)} %bitcast.7), custom_call_target="tpu_custom_call" | custom-call | tf_op jit(solution)/shard_map/spectra/pallas_call | solution.py:120
  4.1 7.3 %all-to-all-start = ((bf16[8,96,384]{2,1,0:T(8,128)(2,1)}), bf16[8,96,384]{2,1,0:T(8,128)(2,1)S(1)}, u32[]{:S(2)}, u32[]{:S(2)}) async-start(bf16[8,96,384]{2,1,0:T(8,128)(2,1)} %spectra.1), calls=%async_computation | async-start | bytes 1179648 | tf_op jit(solution)/shard_map/all_to_all | solution.py:552
  11.4 0.7 or_select_fusion
  12.1 0.8 convert_reduce_fusion.2.start_ref
  12.9 0.6 slice.11.count_ref
  13.6 0.6 convert_reduce_fusion.1
  14.1 0.6 convert_reduce_fusion
  14.7 1.0 %select_reduce_fusion = (s32[1024]{0:T(1024)S(1)}, s32[1024]{0:T(1024)S(1)}) fusion(s32[1024]{0:T(1024)S(1)} %convert_reduce_fusion, s32[1024]{0:T(1024)S(1)} %get-tuple-element.23, s32[1024]{0:T(1024)S(1)} %get-tuple-element.24, s32[1024]{0:T(1024)S(1)} %convert_reduce_fusion.1), kind=kLoop, calls=%fused_computation | loop fusion | flops 6289408 | bytes 24576 | tf_op jit(solution)/shard_map/reduce_sum | solution.py:509
  15.7 0.0 copy-start
  15.7 0.9 %copy-done = f32[180,90,2]{1,2,0:T(2,128)S(1)} copy-done((f32[180,90,2]{1,2,0:T(2,128)S(1)}, f32[180,90,2]{1,2,0:T(2,128)}, u32[]{:S(2)}) %copy-start) | copy-done | bytes 129624
  16.6 2.6 %nuggets.1.nug_ref = f32[8,128]{1,0:T(8,128)S(1)} custom-call(s32[1024]{0:T(1024)S(1)} %get-tuple-element.26.key_ref, s32[1]{0:T(128)} %slice.11.count_ref, f32[180,2,90]{2,1,0:T(2,128)S(1)} %bitcast.5), custom_call_target="tpu_custom_call" | custom-call | tf_op jit(solution)/shard_map/nuggets/pallas_call | solution.py:275
  19.3 0.2 convert_reduce_fusion.3
  19.5 0.1 pad_add_fusion.meta_ref
  19.6 7.7 %all-to-all-done.x_ref = bf16[8,96,384]{2,1,0:T(8,128)(2,1)S(1)} async-done(((bf16[8,96,384]{2,1,0:T(8,128)(2,1)}), bf16[8,96,384]{2,1,0:T(8,128)(2,1)S(1)}, u32[]{:S(2)}, u32[]{:S(2)}) %all-to-all-start) | async-done | bytes 589856 | tf_op jit(solution)/shard_map/all_to_all | solution.py:552
  27.3 15.4 %partials.1 = (bf16[2,184,1536]{2,1,0:T(8,128)(2,1)S(1)}, bf16[2,184,1536]{2,1,0:T(8,128)(2,1)S(1)}, f32[9,8,128]{2,1,0:T(8,128)S(1)}) custom-call(s32[1024]{0:T(1024)S(1)} %get-tuple-element.25.key_ref, s32[9]{0:T(128)S(1)} %pad_add_fusion.meta_ref, bf16[8,96,384]{2,1,0:T(8,128)(2,1)S(1)} %all-to-all-done.x_ref, bf16[90,180,720]{2,1,0:T(8,128)(2,1)} %bitcast.6, ...), custom_call_target="tpu_custom_call" | custom-call | tf_op jit(solution)/shard_map/partials/pallas_call | solution.py:222
  42.7 0.1 collective-permute-start
  42.7 1.2 %collective-permute-done = f32[9,8,128]{2,1,0:T(8,128)S(1)} collective-permute-done((f32[9,8,128]{2,1,0:T(8,128)S(1)}, f32[9,8,128]{2,1,0:T(8,128)S(1)}, u32[]{:S(2)}, u32[]{:S(2)}) %collective-permute-start) | collective-permute-done | bytes 36896 | tf_op jit(solution)/shard_map/ppermute | solution.py:555
  44.0 0.2 collective-permute-start.1
  44.1 1.5 %collective-permute-start.2 = (f32[9,8,128]{2,1,0:T(8,128)S(1)}, f32[9,8,128]{2,1,0:T(8,128)S(1)}, u32[]{:S(2)}, u32[]{:S(2)}) collective-permute-start(f32[9,8,128]{2,1,0:T(8,128)S(1)} %add.36), channel_id=1, source_target_pairs={{0,2},{1,3},{2,0},{3,1},{4,6},{5,7},{6,4},{7,5},{8,10},{9,11},{10,... | collective-permute-start | bytes 110600 | tf_op jit(solution)/shard_map/ppermute | solution.py:559
  45.6 2.4 %collective-permute-done.2 = f32[9,8,128]{2,1,0:T(8,128)S(1)} collective-permute-done((f32[9,8,128]{2,1,0:T(8,128)S(1)}, f32[9,8,128]{2,1,0:T(8,128)S(1)}, u32[]{:S(2)}, u32[]{:S(2)}) %collective-permute-start.2) | collective-permute-done | bytes 36896 | tf_op jit(solution)/shard_map/ppermute | solution.py:559
  48.1 0.0 collective-permute-done.1.refs_1_
  48.1 0.1 add_convert_fusion
  48.2 1.6 %collective-permute-start.3 = (bf16[1,184,1536]{2,1,0:T(8,128)(2,1)S(1)}, bf16[1,184,1536]{2,1,0:T(8,128)(2,1)S(1)}, u32[]{:S(2)}, u32[]{:S(2)}) collective-permute-start(bf16[1,184,1536]{2,1,0:T(8,128)(2,1)S(1)} %add_convert_fusion), channel_id=1, source_target_pairs={{0,2},{1,3},{2,0},{3,1},{4,6},{5,7},{6,4},{7,5},{8,10},{9,11},{10,... | collective-permute-start | bytes 1695752 | tf_op jit(solution)/shard_map/ppermute | solution.py:563
  49.8 1.2 %collective-permute-start.4 = (f32[9,8,128]{2,1,0:T(8,128)S(1)}, f32[9,8,128]{2,1,0:T(8,128)S(1)}, u32[]{:S(2)}, u32[]{:S(2)}) collective-permute-start(f32[9,8,128]{2,1,0:T(8,128)S(1)} %add.38), channel_id=1, source_target_pairs={{0,4},{4,0},{8,12},{12,8},{16,20},{20,16},{24,28},{28,24},{1,5},{5... | collective-permute-start | bytes 110600 | tf_op jit(solution)/shard_map/ppermute | solution.py:565
  51.0 2.8 %collective-permute-done.4 = f32[9,8,128]{2,1,0:T(8,128)S(1)} collective-permute-done((f32[9,8,128]{2,1,0:T(8,128)S(1)}, f32[9,8,128]{2,1,0:T(8,128)S(1)}, u32[]{:S(2)}, u32[]{:S(2)}) %collective-permute-start.4) | collective-permute-done | bytes 36896 | tf_op jit(solution)/shard_map/ppermute | solution.py:565
  53.8 0.2 collective-permute-start.5
  53.9 3.8 %collective-permute-done.5 = f32[9,8,128]{2,1,0:T(8,128)S(1)} collective-permute-done((f32[9,8,128]{2,1,0:T(8,128)S(1)}, f32[9,8,128]{2,1,0:T(8,128)S(1)}, u32[]{:S(2)}, u32[]{:S(2)}) %collective-permute-start.5) | collective-permute-done | bytes 36896 | tf_op jit(solution)/shard_map/ppermute | solution.py:565
  57.8 0.0 collective-permute-start.6
  57.8 5.2 %collective-permute-done.6 = f32[9,8,128]{2,1,0:T(8,128)S(1)} collective-permute-done((f32[9,8,128]{2,1,0:T(8,128)S(1)}, f32[9,8,128]{2,1,0:T(8,128)S(1)}, u32[]{:S(2)}, u32[]{:S(2)}) %collective-permute-start.6) | collective-permute-done | bytes 36896 | tf_op jit(solution)/shard_map/ppermute | solution.py:565
  63.0 0.4 factor.1
  63.4 0.0 collective-permute-done.3.refs_2_
  63.4 27.5 %panels.1 = bf16[180,90,2,1024]{3,2,1,0:T(2,128)(2,1)} custom-call(s32[1024]{0:T(1024)S(1)} %get-tuple-element.26.key_ref, s32[11]{0:T(128)S(1)} %convert_reduce_fusion.2.start_ref, bf16[2,184,1536]{2,1,0:T(8,128)(2,1)S(1)} %get-tuple-element.14.refs_0_, bf16[2,184,1536]{2,1,0:T(8,128)(2,1)S(1)} %collective-permute-done.1.refs_1_, ...), custom_call_target="tpu_custom_call" | custom-call | tf_op jit(solution)/shard_map/panels/pallas_call | solution.py:486
  (10 shorter events, 0.0 us)
Async XLA Ops:
  4.1 23.2 %all-to-all-start = ((bf16[8,96,384]{2,1,0:T(8,128)(2,1)}), bf16[8,96,384]{2,1,0:T(8,128)(2,1)S(1)}, u32[]{:S(2)}, u32[]{:S(2)}) async-start(bf16[8,96,384]{2,1,0:T(8,128)(2,1)} %spectra.1), calls=%async_computation | async-start | bytes 1179648 | tf_op jit(solution)/shard_map/all_to_all | solution.py:552
  15.7 0.9 %copy-start = (f32[180,90,2]{1,2,0:T(2,128)S(1)}, f32[180,90,2]{1,2,0:T(2,128)}, u32[]{:S(2)}) copy-start(f32[180,90,2]{1,2,0:T(2,128)} %param.10) | copy-start | bytes 388804
  27.3 35.7 %copy-start.1 = (bf16[128,256]{1,0:T(8,128)(2,1)S(1)}, bf16[128,256]{1,0:T(8,128)(2,1)}, u32[]{:S(2)}) copy-start(bf16[128,256]{1,0:T(8,128)(2,1)} %constant.77.clone.tri_ref) | copy-start | bytes 196612
  27.3 36.1 %copy-start.2 = (bf16[5,16,128]{2,1,0:T(8,128)(2,1)S(1)}, bf16[5,16,128]{2,1,0:T(8,128)(2,1)}, u32[]{:S(2)}) copy-start(bf16[5,16,128]{2,1,0:T(8,128)(2,1)} %constant.78.clone.refs_3_) | copy-start | bytes 61444
  42.7 1.3 %collective-permute-start = (f32[9,8,128]{2,1,0:T(8,128)S(1)}, f32[9,8,128]{2,1,0:T(8,128)S(1)}, u32[]{:S(2)}, u32[]{:S(2)}) collective-permute-start(f32[9,8,128]{2,1,0:T(8,128)S(1)} %get-tuple-element.16), channel_id=1, source_target_pairs={{0,1},{1,0},{2,3},{3,2},{4,5},{5,4},{6,7},{7,6},{8,9},{9,8},{10,11... | collective-permute-start | bytes 110600 | tf_op jit(solution)/shard_map/ppermute | solution.py:555
  44.0 4.1 %collective-permute-start.1 = (bf16[2,184,1536]{2,1,0:T(8,128)(2,1)S(1)}, bf16[2,184,1536]{2,1,0:T(8,128)(2,1)S(1)}, u32[]{:S(2)}, u32[]{:S(2)}) collective-permute-start(bf16[2,184,1536]{2,1,0:T(8,128)(2,1)S(1)} %get-tuple-element.17), channel_id=1, source_target_pairs={{0,1},{1,0},{2,3},{3,2},{4,5},{5,4},{6,7},{7,6},{8,9},{9,8},{10,11... | collective-permute-start | bytes 3391496 | tf_op jit(solution)/shard_map/ppermute | solution.py:557
  44.1 4.0 %collective-permute-start.2 = (f32[9,8,128]{2,1,0:T(8,128)S(1)}, f32[9,8,128]{2,1,0:T(8,128)S(1)}, u32[]{:S(2)}, u32[]{:S(2)}) collective-permute-start(f32[9,8,128]{2,1,0:T(8,128)S(1)} %add.36), channel_id=1, source_target_pairs={{0,2},{1,3},{2,0},{3,1},{4,6},{5,7},{6,4},{7,5},{8,10},{9,11},{10,... | collective-permute-start | bytes 110600 | tf_op jit(solution)/shard_map/ppermute | solution.py:559
  48.2 15.2 %collective-permute-start.3 = (bf16[1,184,1536]{2,1,0:T(8,128)(2,1)S(1)}, bf16[1,184,1536]{2,1,0:T(8,128)(2,1)S(1)}, u32[]{:S(2)}, u32[]{:S(2)}) collective-permute-start(bf16[1,184,1536]{2,1,0:T(8,128)(2,1)S(1)} %add_convert_fusion), channel_id=1, source_target_pairs={{0,2},{1,3},{2,0},{3,1},{4,6},{5,7},{6,4},{7,5},{8,10},{9,11},{10,... | collective-permute-start | bytes 1695752 | tf_op jit(solution)/shard_map/ppermute | solution.py:563
  49.8 4.0 %collective-permute-start.4 = (f32[9,8,128]{2,1,0:T(8,128)S(1)}, f32[9,8,128]{2,1,0:T(8,128)S(1)}, u32[]{:S(2)}, u32[]{:S(2)}) collective-permute-start(f32[9,8,128]{2,1,0:T(8,128)S(1)} %add.38), channel_id=1, source_target_pairs={{0,4},{4,0},{8,12},{12,8},{16,20},{20,16},{24,28},{28,24},{1,5},{5... | collective-permute-start | bytes 110600 | tf_op jit(solution)/shard_map/ppermute | solution.py:565
  53.8 4.0 %collective-permute-start.5 = (f32[9,8,128]{2,1,0:T(8,128)S(1)}, f32[9,8,128]{2,1,0:T(8,128)S(1)}, u32[]{:S(2)}, u32[]{:S(2)}) collective-permute-start(f32[9,8,128]{2,1,0:T(8,128)S(1)} %add.39), channel_id=1, source_target_pairs={{0,8},{4,12},{8,0},{12,4},{16,24},{20,28},{24,16},{28,20},{1,9},{5... | collective-permute-start | bytes 110600 | tf_op jit(solution)/shard_map/ppermute | solution.py:565
  57.8 5.2 %collective-permute-start.6 = (f32[9,8,128]{2,1,0:T(8,128)S(1)}, f32[9,8,128]{2,1,0:T(8,128)S(1)}, u32[]{:S(2)}, u32[]{:S(2)}) collective-permute-start(f32[9,8,128]{2,1,0:T(8,128)S(1)} %add.40), channel_id=1, source_target_pairs={{0,16},{4,20},{8,24},{12,28},{16,0},{20,4},{24,8},{28,12},{1,17},{... | collective-permute-start | bytes 110600 | tf_op jit(solution)/shard_map/ppermute | solution.py:565

commit v4 on v3

--- a/solution.py
+++ b/solution.py
@@ -11,8 +11,7 @@
 
 LANE = 128
 ROWS = 16
-DESTS = 8
-GROUP = 16
+GROUP = 32
 VMEM = 48 << 20
 MOST = 58 << 20
 F32, BF16 = jnp.float32, jnp.bfloat16
@@ -63,26 +62,24 @@
 
 
 def spectra_kernel(n_lon, ords, rows, f_hbm, o_ref, table, f_ref, sem):
-    step = pl.program_id(0)
     per = o_ref.shape[0]
     lats = f_ref.shape[0]
     tiles = rows // 8
-
-    @pl.when(step == 0)
-    def _():
-        pltpu.make_async_copy(f_hbm, f_ref, sem).start()
+    fields_in = pltpu.make_async_copy(f_hbm, f_ref, sem)
+    fields_in.start()
 
     shape = (per * tiles, 2 * LANE)
     lane = lax.broadcasted_iota(jnp.int32, shape, 1)
     lane = jnp.minimum(lane, LANE).astype(F32)
     tile = lax.broadcasted_iota(jnp.int32, shape, 0)
     of = sum((tile >= tiles * d).astype(jnp.int32) for d in range(1, per)) if per > 1 else 0
-    first = ((step * per + of) * ords + 8 * (tile - tiles * of)).astype(F32)
+    first = (of * ords + 8 * (tile - tiles * of)).astype(F32)
     pc, ps = turn(first * lane, n_lon)
     few = lax.broadcasted_iota(jnp.int32, (8, 2 * LANE), 0).astype(F32)
     qc, qs = turn(few * lane[:1], n_lon)
     scale = 1.0 / math.sqrt(n_lon)
-    for p in range(0, per * tiles, 2):
+
+    def fill(p):
         both_c, both_s = [], []
         for i in (p, p + 1):
             both_c.append(pc[i : i + 1] * qc - ps[i : i + 1] * qs)
@@ -100,28 +97,34 @@
             table[at_s : at_s + 16, at] = (-s[:, :width]).astype(BF16)
             c, s = c * rc - s * rs, s * rc + c * rs
 
-    @pl.when(step == 0)
-    def _():
-        pltpu.make_async_copy(f_hbm, f_ref, sem).wait()
-
+    some = divisor(per, max(per // 2, 1))
     pad = jnp.zeros((rows, o_ref.shape[2] - 2 * lats), F32)
-    y = lax.dot_general(table[...], f_ref[...], NT, preferred_element_type=F32)
-    for d in range(per):
-        re = y[2 * d * rows : (2 * d + 1) * rows]
-        im = y[(2 * d + 1) * rows : (2 * d + 2) * rows]
-        o_ref[d] = jnp.concatenate([re, im, pad], axis=1).astype(BF16)
+    for q in range(per // some + 1):
+        if q < per // some:
+            for p in range(q * some * tiles, (q + 1) * some * tiles, 2):
+                fill(p)
+        if q == 0:
+            fields_in.wait()
+            continue
+        at = (q - 1) * some
+        y = lax.dot_general(
+            table[2 * at * rows : 2 * (at + some) * rows, :], f_ref[...], NT, preferred_element_type=F32
+        )
+        for d in range(some):
+            re = y[2 * d * rows : (2 * d + 1) * rows]
+            im = y[(2 * d + 1) * rows : (2 * d + 2) * rows]
+            o_ref[at + d] = jnp.concatenate([re, im, pad], axis=1).astype(BF16)
 
 
 def spectra(fields, ords, dests):
     lats, n_lon = fields.shape
     rows = div_up(ords, GROUP) * GROUP
     lanes = div_up(2 * lats, LANE) * LANE
-    per = divisor(dests, DESTS)
+    per = dests
     return pl.pallas_call(
         functools.partial(spectra_kernel, n_lon, ords, rows),
-        grid=(dests // per,),
         in_specs=[pl.BlockSpec(memory_space=pl.ANY)],
-        out_specs=pl.BlockSpec((per, rows, lanes), lambda i: (i, 0, 0)),
+        out_specs=pl.BlockSpec(memory_space=pltpu.VMEM),
         out_shape=jax.ShapeDtypeStruct((dests, rows, lanes), BF16),
         scratch_shapes=[
             pltpu.VMEM((2 * per * rows, n_lon), BF16),
@@ -162,7 +165,7 @@
         row = jnp.concatenate([re[at], im[at]], axis=0).astype(BF16)
         y = jnp.dot(row, leg_ref[r], preferred_element_type=F32)
         least = ord_start + step * GROUP + r
-        flat[width * r : width * (r + 1), :degs] = jnp.where(deg >= least, y, 0.0).astype(BF16).astype(F32)
+        flat[width * r : width * (r + 1), :degs] = jnp.where(deg >= least, y, 0.0).astype(BF16)
 
     full = ords - (div_up(ords, GROUP) - 1) * GROUP
     for r in range(full):
@@ -173,7 +176,7 @@
         for r in range(full, GROUP):
             order_rows(r)
 
-    turned[...] = flat[...].T
+    turned[...] = flat[...].T.astype(F32)
     for d in range(blocks):
         part = turned[deg_local * d : deg_local * (d + 1), :].astype(BF16)
         where = d ^ me
@@ -235,7 +238,7 @@
                 pl.BlockSpec((times + 1, cols // LANE, LANE), lambda i, *_: (0, 0, 0)),
             ],
             scratch_shapes=[
-                pltpu.VMEM((lanes, div_up(degs, LANE) * LANE), F32),
+                pltpu.VMEM((lanes, div_up(degs, LANE) * LANE), BF16),
                 pltpu.VMEM((div_up(degs, LANE) * LANE, lanes), F32),
                 pltpu.VMEM((cols, lanes), F32),
             ],

time: 91.3 us -> 89.3 us (0.978)
  Pallas kernels: 50 us -> 48 us
    pallas_call x1, Pallas kernels: 15.4 us -> 14.2 us  [partials(): pl.pallas_call(functools.partial(partial_kernel, dims), grid_spec=pltpu.P...]
where the time goes in v4:
time: 89.3 us; the launch traced here: 89.1 us
  Pallas kernels  48 us (54%)
  waiting for transfers between devices  23.3 us (26%)
  starting transfers between devices  11.9 us (13%)
  other arithmetic  4.15 us (5%)
  local copies, waits for them, and re-layouts  1.54 us (2%)
    pallas_call x1, Pallas kernels, panels(): pl.pallas_call(functools.partial(panel_kernel, dims, len(parts)), grid_sp...  27.4 us
    pallas_call x1, Pallas kernels, partials(): pl.pallas_call(functools.partial(partial_kernel, dims), grid_spec=pltpu.P...  14.2 us
    ppermute x3, waiting for transfers between devices, on_device(): picks = picks + lax.ppermute(picks, 'tm', partner('tm', bit))  11.9 us
    all_to_all x1, waiting for transfers between devices, on_device(): moved = lax.all_to_all(sent, 'tm', split_axis=0, concat_axis=0, tiled=True)  7.8 us
    all_to_all x1, starting transfers between devices, on_device(): moved = lax.all_to_all(sent, 'tm', split_axis=0, concat_axis=0, tiled=True)  7.26 us
    pallas_call x1, Pallas kernels, spectra(): pl.pallas_call(functools.partial(spectra_kernel, n_lon, ords, rows), in_s...  3.37 us
    pallas_call x1, Pallas kernels, nuggets_of(): pl.pallas_call(functools.partial(nugget_kernel, (ords, cols)), grid_spec=...  2.56 us
    ppermute x1, waiting for transfers between devices, on_device(): picks = picks + lax.ppermute(picks, 'lat', partner('lat', bit))  2.44 us
  transfers between devices with their start and end apart: 8, of which 6 were waited for; matrix products, arithmetic and copies ran while one was open for 5% of the time, Pallas kernels for 3%

profile of v4, /device:TPU:0, one launch (start us, length us, event | category | flops | bytes accessed | tf_op | source)
XLA Modules:
  0.0 89.1 jit_solution(11487143878334175932)
XLA Ops:
  0.0 3.4 %spectra.1 = bf16[8,96,384]{2,1,0:T(8,128)(2,1)} custom-call(bf16[180,1440]{1,0:T(8,128)(2,1)} %bitcast.7), custom_call_target="tpu_custom_call" | custom-call | tf_op jit(solution)/shard_map/spectra/pallas_call | solution.py:124
  3.4 7.3 %all-to-all-start = ((bf16[8,96,384]{2,1,0:T(8,128)(2,1)}), bf16[8,96,384]{2,1,0:T(8,128)(2,1)S(1)}, u32[]{:S(2)}, u32[]{:S(2)}) async-start(bf16[8,96,384]{2,1,0:T(8,128)(2,1)} %spectra.1), calls=%async_computation | async-start | bytes 1179648 | tf_op jit(solution)/shard_map/all_to_all | solution.py:555
  10.6 0.7 or_select_fusion
  11.4 0.8 convert_reduce_fusion.2.start_ref
  12.2 0.6 slice.11.count_ref
  12.8 0.6 convert_reduce_fusion.1
  13.4 0.6 convert_reduce_fusion
  13.9 1.0 %select_reduce_fusion = (s32[1024]{0:T(1024)S(1)}, s32[1024]{0:T(1024)S(1)}) fusion(s32[1024]{0:T(1024)S(1)} %convert_reduce_fusion, s32[1024]{0:T(1024)S(1)} %get-tuple-element.23, s32[1024]{0:T(1024)S(1)} %get-tuple-element.24, s32[1024]{0:T(1024)S(1)} %convert_reduce_fusion.1), kind=kLoop, calls=%fused_computation | loop fusion | flops 6289408 | bytes 24576 | tf_op jit(solution)/shard_map/reduce_sum | solution.py:512
  15.0 0.0 copy-start
  15.0 0.9 %copy-done = f32[180,90,2]{1,2,0:T(2,128)S(1)} copy-done((f32[180,90,2]{1,2,0:T(2,128)S(1)}, f32[180,90,2]{1,2,0:T(2,128)}, u32[]{:S(2)}) %copy-start) | copy-done | bytes 129624
  15.9 2.6 %nuggets.1.nug_ref = f32[8,128]{1,0:T(8,128)S(1)} custom-call(s32[1024]{0:T(1024)S(1)} %get-tuple-element.26.key_ref, s32[1]{0:T(128)} %slice.11.count_ref, f32[180,2,90]{2,1,0:T(2,128)S(1)} %bitcast.5), custom_call_target="tpu_custom_call" | custom-call | tf_op jit(solution)/shard_map/nuggets/pallas_call | solution.py:278
  18.5 0.2 convert_reduce_fusion.3
  18.7 0.1 pad_add_fusion.meta_ref
  18.7 7.8 %all-to-all-done.x_ref = bf16[8,96,384]{2,1,0:T(8,128)(2,1)S(1)} async-done(((bf16[8,96,384]{2,1,0:T(8,128)(2,1)}), bf16[8,96,384]{2,1,0:T(8,128)(2,1)S(1)}, u32[]{:S(2)}, u32[]{:S(2)}) %all-to-all-start) | async-done | bytes 589856 | tf_op jit(solution)/shard_map/all_to_all | solution.py:555
  26.5 14.2 %partials.1 = (bf16[2,184,1536]{2,1,0:T(8,128)(2,1)S(1)}, bf16[2,184,1536]{2,1,0:T(8,128)(2,1)S(1)}, f32[9,8,128]{2,1,0:T(8,128)S(1)}) custom-call(s32[1024]{0:T(1024)S(1)} %get-tuple-element.25.key_ref, s32[6]{0:T(128)S(1)} %pad_add_fusion.meta_ref, bf16[8,96,384]{2,1,0:T(8,128)(2,1)S(1)} %all-to-all-done.x_ref, bf16[90,180,720]{2,1,0:T(8,128)(2,1)} %bitcast.6, ...), custom_call_target="tpu_custom_call" | custom-call | tf_op jit(solution)/shard_map/partials/pallas_call | solution.py:225
  40.7 0.1 collective-permute-start
  40.8 1.2 %collective-permute-done = f32[9,8,128]{2,1,0:T(8,128)S(1)} collective-permute-done((f32[9,8,128]{2,1,0:T(8,128)S(1)}, f32[9,8,128]{2,1,0:T(8,128)S(1)}, u32[]{:S(2)}, u32[]{:S(2)}) %collective-permute-start) | collective-permute-done | bytes 36896 | tf_op jit(solution)/shard_map/ppermute | solution.py:558
  42.0 0.2 collective-permute-start.1
  42.2 1.5 %collective-permute-start.2 = (f32[9,8,128]{2,1,0:T(8,128)S(1)}, f32[9,8,128]{2,1,0:T(8,128)S(1)}, u32[]{:S(2)}, u32[]{:S(2)}) collective-permute-start(f32[9,8,128]{2,1,0:T(8,128)S(1)} %add.36), channel_id=1, source_target_pairs={{0,2},{1,3},{2,0},{3,1},{4,6},{5,7},{6,4},{7,5},{8,10},{9,11},{10,... | collective-permute-start | bytes 110600 | tf_op jit(solution)/shard_map/ppermute | solution.py:562
  43.7 2.4 %collective-permute-done.2 = f32[9,8,128]{2,1,0:T(8,128)S(1)} collective-permute-done((f32[9,8,128]{2,1,0:T(8,128)S(1)}, f32[9,8,128]{2,1,0:T(8,128)S(1)}, u32[]{:S(2)}, u32[]{:S(2)}) %collective-permute-start.2) | collective-permute-done | bytes 36896 | tf_op jit(solution)/shard_map/ppermute | solution.py:562
  46.2 0.0 collective-permute-done.1.refs_1_
  46.2 0.1 add_convert_fusion
  46.3 1.6 %collective-permute-start.3 = (bf16[1,184,1536]{2,1,0:T(8,128)(2,1)S(1)}, bf16[1,184,1536]{2,1,0:T(8,128)(2,1)S(1)}, u32[]{:S(2)}, u32[]{:S(2)}) collective-permute-start(bf16[1,184,1536]{2,1,0:T(8,128)(2,1)S(1)} %add_convert_fusion), channel_id=1, source_target_pairs={{0,2},{1,3},{2,0},{3,1},{4,6},{5,7},{6,4},{7,5},{8,10},{9,11},{10,... | collective-permute-start | bytes 1695752 | tf_op jit(solution)/shard_map/ppermute | solution.py:566
  47.9 1.0 %collective-permute-start.4 = (f32[9,8,128]{2,1,0:T(8,128)S(1)}, f32[9,8,128]{2,1,0:T(8,128)S(1)}, u32[]{:S(2)}, u32[]{:S(2)}) collective-permute-start(f32[9,8,128]{2,1,0:T(8,128)S(1)} %add.38), channel_id=1, source_target_pairs={{0,4},{4,0},{8,12},{12,8},{16,20},{20,16},{24,28},{28,24},{1,5},{5... | collective-permute-start | bytes 110600 | tf_op jit(solution)/shard_map/ppermute | solution.py:568
  48.9 2.9 %collective-permute-done.4 = f32[9,8,128]{2,1,0:T(8,128)S(1)} collective-permute-done((f32[9,8,128]{2,1,0:T(8,128)S(1)}, f32[9,8,128]{2,1,0:T(8,128)S(1)}, u32[]{:S(2)}, u32[]{:S(2)}) %collective-permute-start.4) | collective-permute-done | bytes 36896 | tf_op jit(solution)/shard_map/ppermute | solution.py:568
  51.9 0.2 collective-permute-start.5
  52.1 3.7 %collective-permute-done.5 = f32[9,8,128]{2,1,0:T(8,128)S(1)} collective-permute-done((f32[9,8,128]{2,1,0:T(8,128)S(1)}, f32[9,8,128]{2,1,0:T(8,128)S(1)}, u32[]{:S(2)}, u32[]{:S(2)}) %collective-permute-start.5) | collective-permute-done | bytes 36896 | tf_op jit(solution)/shard_map/ppermute | solution.py:568
  55.8 0.0 collective-permute-start.6
  55.8 5.2 %collective-permute-done.6 = f32[9,8,128]{2,1,0:T(8,128)S(1)} collective-permute-done((f32[9,8,128]{2,1,0:T(8,128)S(1)}, f32[9,8,128]{2,1,0:T(8,128)S(1)}, u32[]{:S(2)}, u32[]{:S(2)}) %collective-permute-start.6) | collective-permute-done | bytes 36896 | tf_op jit(solution)/shard_map/ppermute | solution.py:568
  61.1 0.4 factor.1
  61.5 0.0 collective-permute-done.3.refs_2_
  61.5 27.4 %panels.1 = bf16[180,90,2,1024]{3,2,1,0:T(2,128)(2,1)} custom-call(s32[1024]{0:T(1024)S(1)} %get-tuple-element.26.key_ref, s32[11]{0:T(128)S(1)} %convert_reduce_fusion.2.start_ref, bf16[2,184,1536]{2,1,0:T(8,128)(2,1)S(1)} %get-tuple-element.14.refs_0_, bf16[2,184,1536]{2,1,0:T(8,128)(2,1)S(1)} %collective-permute-done.1.refs_1_, ...), custom_call_target="tpu_custom_call" | custom-call | tf_op jit(solution)/shard_map/panels/pallas_call | solution.py:489
  (10 shorter events, 0.0 us)
Async XLA Ops:
  3.4 23.2 %all-to-all-start = ((bf16[8,96,384]{2,1,0:T(8,128)(2,1)}), bf16[8,96,384]{2,1,0:T(8,128)(2,1)S(1)}, u32[]{:S(2)}, u32[]{:S(2)}) async-start(bf16[8,96,384]{2,1,0:T(8,128)(2,1)} %spectra.1), calls=%async_computation | async-start | bytes 1179648 | tf_op jit(solution)/shard_map/all_to_all | solution.py:555
  15.0 0.9 %copy-start = (f32[180,90,2]{1,2,0:T(2,128)S(1)}, f32[180,90,2]{1,2,0:T(2,128)}, u32[]{:S(2)}) copy-start(f32[180,90,2]{1,2,0:T(2,128)} %param.10) | copy-start | bytes 388804
  26.5 34.6 %copy-start.1 = (bf16[128,256]{1,0:T(8,128)(2,1)S(1)}, bf16[128,256]{1,0:T(8,128)(2,1)}, u32[]{:S(2)}) copy-start(bf16[128,256]{1,0:T(8,128)(2,1)} %constant.77.clone.tri_ref) | copy-start | bytes 196612
  26.5 35.0 %copy-start.2 = (bf16[5,16,128]{2,1,0:T(8,128)(2,1)S(1)}, bf16[5,16,128]{2,1,0:T(8,128)(2,1)}, u32[]{:S(2)}) copy-start(bf16[5,16,128]{2,1,0:T(8,128)(2,1)} %constant.78.clone.refs_3_) | copy-start | bytes 61444
  40.7 1.3 %collective-permute-start = (f32[9,8,128]{2,1,0:T(8,128)S(1)}, f32[9,8,128]{2,1,0:T(8,128)S(1)}, u32[]{:S(2)}, u32[]{:S(2)}) collective-permute-start(f32[9,8,128]{2,1,0:T(8,128)S(1)} %get-tuple-element.16), channel_id=1, source_target_pairs={{0,1},{1,0},{2,3},{3,2},{4,5},{5,4},{6,7},{7,6},{8,9},{9,8},{10,11... | collective-permute-start | bytes 110600 | tf_op jit(solution)/shard_map/ppermute | solution.py:558
  42.0 4.1 %collective-permute-start.1 = (bf16[2,184,1536]{2,1,0:T(8,128)(2,1)S(1)}, bf16[2,184,1536]{2,1,0:T(8,128)(2,1)S(1)}, u32[]{:S(2)}, u32[]{:S(2)}) collective-permute-start(bf16[2,184,1536]{2,1,0:T(8,128)(2,1)S(1)} %get-tuple-element.17), channel_id=1, source_target_pairs={{0,1},{1,0},{2,3},{3,2},{4,5},{5,4},{6,7},{7,6},{8,9},{9,8},{10,11... | collective-permute-start | bytes 3391496 | tf_op jit(solution)/shard_map/ppermute | solution.py:560
  42.2 4.0 %collective-permute-start.2 = (f32[9,8,128]{2,1,0:T(8,128)S(1)}, f32[9,8,128]{2,1,0:T(8,128)S(1)}, u32[]{:S(2)}, u32[]{:S(2)}) collective-permute-start(f32[9,8,128]{2,1,0:T(8,128)S(1)} %add.36), channel_id=1, source_target_pairs={{0,2},{1,3},{2,0},{3,1},{4,6},{5,7},{6,4},{7,5},{8,10},{9,11},{10,... | collective-permute-start | bytes 110600 | tf_op jit(solution)/shard_map/ppermute | solution.py:562
  46.3 15.2 %collective-permute-start.3 = (bf16[1,184,1536]{2,1,0:T(8,128)(2,1)S(1)}, bf16[1,184,1536]{2,1,0:T(8,128)(2,1)S(1)}, u32[]{:S(2)}, u32[]{:S(2)}) collective-permute-start(bf16[1,184,1536]{2,1,0:T(8,128)(2,1)S(1)} %add_convert_fusion), channel_id=1, source_target_pairs={{0,2},{1,3},{2,0},{3,1},{4,6},{5,7},{6,4},{7,5},{8,10},{9,11},{10,... | collective-permute-start | bytes 1695752 | tf_op jit(solution)/shard_map/ppermute | solution.py:566
  47.9 4.0 %collective-permute-start.4 = (f32[9,8,128]{2,1,0:T(8,128)S(1)}, f32[9,8,128]{2,1,0:T(8,128)S(1)}, u32[]{:S(2)}, u32[]{:S(2)}) collective-permute-start(f32[9,8,128]{2,1,0:T(8,128)S(1)} %add.38), channel_id=1, source_target_pairs={{0,4},{4,0},{8,12},{12,8},{16,20},{20,16},{24,28},{28,24},{1,5},{5... | collective-permute-start | bytes 110600 | tf_op jit(solution)/shard_map/ppermute | solution.py:568
  51.9 4.0 %collective-permute-start.5 = (f32[9,8,128]{2,1,0:T(8,128)S(1)}, f32[9,8,128]{2,1,0:T(8,128)S(1)}, u32[]{:S(2)}, u32[]{:S(2)}) collective-permute-start(f32[9,8,128]{2,1,0:T(8,128)S(1)} %add.39), channel_id=1, source_target_pairs={{0,8},{4,12},{8,0},{12,4},{16,24},{20,28},{24,16},{28,20},{1,9},{5... | collective-permute-start | bytes 110600 | tf_op jit(solution)/shard_map/ppermute | solution.py:568
  55.8 5.3 %collective-permute-start.6 = (f32[9,8,128]{2,1,0:T(8,128)S(1)}, f32[9,8,128]{2,1,0:T(8,128)S(1)}, u32[]{:S(2)}, u32[]{:S(2)}) collective-permute-start(f32[9,8,128]{2,1,0:T(8,128)S(1)} %add.40), channel_id=1, source_target_pairs={{0,16},{4,20},{8,24},{12,28},{16,0},{20,4},{24,8},{28,12},{1,17},{... | collective-permute-start | bytes 110600 | tf_op jit(solution)/shard_map/ppermute | solution.py:568
